TPU v7x, 512 devices: a whole 4x8x8 slice. The times are simulated.
512 devices in a mesh: blk: 16 (over z_lo, y), group: 32 (over z_hi, x, core).
Axes of the slice: x: 4, y: 8, z: 8 (z_hi: 4, z_lo: 2; z = z_hi * 2 + z_lo), core: 2. Of those that a mesh axis runs over, the one named last changes fastest.
Arguments:
- audio: bfloat16 [81920, 1024], P(('blk', 'group')), may hold values from -3 to 3
- text: bfloat16 [81920, 768], P(('blk', 'group')), may hold values from -4 to 4
- labels: int32 [81920], P(('blk', 'group')), may hold values from 0 to 319
- audio_weight: bfloat16 [1024, 768], P('group'), may hold values from -0.1875 to 0.1875
Outputs:
- audio_grad: bfloat16 [81920, 1024], P(('blk', 'group'))
- text_grad: bfloat16 [81920, 768], P(('blk', 'group'))
- weight_grad: float32 [1024, 768], P('group')
All inputs are finite; a program needn't handle non-finite values.
Results may differ from a plain program's by a relative error of at most 0.024.
Values may be sent and summed in bfloat16 or wider, within the bound.
A program may use at most 64 MiB of HBM per device.

v0:
```python
import jax
import jax.numpy as jnp
from jax import lax
from jax.sharding import PartitionSpec as P

SCALE = 16.0
SHIFT = -4.0


def shifted(block, axis, distance):
    devices = range(lax.axis_size(axis))
    route = [((i - distance) % len(devices), i) for i in devices]
    return lax.ppermute(block, axis, route)


def unit_rows(values):
    norm = jnp.sqrt(jnp.sum(values * values, axis=-1, keepdims=True) + 1e-06)
    return (values / norm, norm)


def pair_weights(audio_rows, audio_labels, text_rows, text_labels):
    logits = (
        SCALE
        * lax.dot_general(
            audio_rows, text_rows, (((1,), (1,)), ((), ())), preferred_element_type=jnp.float32
        )
        + SHIFT
    )
    positive = (audio_labels[:, None] == text_labels[None, :]).astype(jnp.float32)
    return (SCALE * (jax.nn.sigmoid(logits) - positive)).astype(jnp.bfloat16)


def block_terms(audio_unit, own_labels, text_rows, text_labels):
    weights = pair_weights(audio_unit, own_labels, text_rows, text_labels)
    d_audio = jnp.dot(weights, text_rows, preferred_element_type=jnp.float32)
    d_text = lax.dot_general(
        weights, audio_unit, (((0,), (0,)), ((), ())), preferred_element_type=jnp.float32
    )
    return (d_audio, d_text)


def on_device(audio, text, labels, audio_weight):
    columns = audio
    proj = jnp.dot(
        columns,
        lax.all_gather(audio_weight, "group", axis=0, tiled=True),
        preferred_element_type=jnp.float32,
    )
    unit_a, norm_a = unit_rows(proj)
    audio_unit = unit_a.astype(jnp.bfloat16)
    unit_t, norm_t = unit_rows(text.astype(jnp.float32))
    text_unit = unit_t.astype(jnp.bfloat16)
    loop_size = lax.axis_size("blk")
    own_audio, own_text = block_terms(audio_unit, labels, text_unit, labels)

    def one_turn(step, state):
        moving_text, moving_labels, carried, d_audio = state
        moving_text, moving_labels = shifted((moving_text, moving_labels), "blk", 1)
        carried = shifted(carried.astype(jnp.bfloat16), "blk", 1).astype(carried.dtype)
        more_audio, more_text = block_terms(audio_unit, labels, moving_text, moving_labels)
        return (moving_text, moving_labels, carried + more_text, d_audio + more_audio)

    state = lax.fori_loop(1, loop_size, one_turn, (text_unit, labels, own_text, own_audio))
    d_audio = state[3]
    text_sum = shifted(state[2].astype(jnp.bfloat16), "blk", 1).astype(jnp.float32)
    dproj = (d_audio - unit_a * jnp.sum(unit_a * d_audio, axis=-1, keepdims=True)) / norm_a
    dproj_low = dproj.astype(jnp.bfloat16)
    audio_back = lax.dot_general(
        dproj_low,
        lax.all_gather(audio_weight, "group", axis=0, tiled=True),
        (((1,), (1,)), ((), ())),
        preferred_element_type=jnp.float32,
    )
    audio_grad = audio_back.astype(jnp.bfloat16)
    columns = audio
    weight_share = lax.psum_scatter(
        lax.dot_general(
            columns, dproj_low, (((0,), (0,)), ((), ())), preferred_element_type=jnp.float32
        ).astype(jnp.bfloat16),
        "group",
        scatter_dimension=0,
        tiled=True,
    )
    weight_grad = lax.psum(weight_share, "blk").astype(jnp.float32)
    text_grad = (
        (text_sum - unit_t * jnp.sum(unit_t * text_sum, axis=-1, keepdims=True)) / norm_t
    ).astype(jnp.bfloat16)
    return (audio_grad, text_grad, weight_grad)


def solution(mesh):
    placed = (
        P(("blk", "group"), None),
        P(("blk", "group"), None),
        P(("blk", "group")),
        P("group", None),
    )
    return jax.shard_map(
        on_device,
        mesh=mesh,
        in_specs=placed,
        out_specs=(P(("blk", "group"), None), P(("blk", "group"), None), P("group", None)),
        check_vma=False,
    )
```

profile of v0, /device:TPU:6, one launch (start us, length us, event | category | flops | bytes accessed | tf_op | source)
XLA Modules:
  0.0 488.2 jit_solution(14412852788563658992)
XLA Ops:
  10.8 62.9 %all-gather.2.cloned.1.call-done = bf16[1024,768]{1,0:T(8,128)(2,1)} async-done(((bf16[32,768]{1,0:T(8,128)(2,1)}), bf16[1024,768]{1,0:T(8,128)(2,1)}) %all-gather.2.cloned.1.call-update) | async-done | bytes 1572880 | tf_op jit(solution)/shard_map/all_gather | solution.py:46
  73.7 1.9 multiply_reduce_fusion.1
  76.6 243.4 %while.16 = (s32[]{:T(128)}, bf16[160,768]{1,0:T(8,128)(2,1)S(1)}, s32[160]{0:T(256)S(1)}, bf16[160,768]{1,0:T(8,128)(2,1)S(1)}, f32[160,768]{1,0:T(8,128)S(1)},...) while((s32[]{:T(128)}, bf16[160,768]{1,0:T(8,128)(2,1)S(1)}, s32[160]{0:T(256)S(1)}, ...), condition=%wide.region_3.0_spmd, body=%wide.region_2.0_spmd.sunk | while | flops 118712320 | bytes 5074125 | solution.py:63
  76.6 3.4 collective-permute-start
  80.0 3.4 collective-permute-start.2
  83.4 3.4 collective-permute-start.1
  86.8 7.3 %collective-permute-done.1 = s32[160]{0:T(256)S(1)} collective-permute-done((s32[160]{0:T(256)S(1)}, s32[160]{0:T(256)S(1)}, u32[]{:S(2)}, u32[]{:S(2)}) %collective-permute-start.1) | collective-permute-done | bytes 672 | tf_op jit(solution)/shard_map/while/body/eval_jaxpr/ppermute | solution.py:13
  94.9 1.9 collective-permute-start
  96.8 2.8 collective-permute-start.2
  99.6 3.6 collective-permute-start.1
  103.2 8.3 %collective-permute-done.1 = s32[160]{0:T(256)S(1)} collective-permute-done((s32[160]{0:T(256)S(1)}, s32[160]{0:T(256)S(1)}, u32[]{:S(2)}, u32[]{:S(2)}) %collective-permute-start.1) | collective-permute-done | bytes 672 | tf_op jit(solution)/shard_map/while/body/eval_jaxpr/ppermute | solution.py:13
  112.3 1.9 collective-permute-start
  114.3 1.9 collective-permute-start.2
  116.2 3.5 collective-permute-start.1
  119.7 8.3 %collective-permute-done.1 = s32[160]{0:T(256)S(1)} collective-permute-done((s32[160]{0:T(256)S(1)}, s32[160]{0:T(256)S(1)}, u32[]{:S(2)}, u32[]{:S(2)}) %collective-permute-start.1) | collective-permute-done | bytes 672 | tf_op jit(solution)/shard_map/while/body/eval_jaxpr/ppermute | solution.py:13
  128.8 1.9 collective-permute-start
  130.8 1.9 collective-permute-start.2
  132.7 2.6 collective-permute-start.1
  135.3 8.2 %collective-permute-done.1 = s32[160]{0:T(256)S(1)} collective-permute-done((s32[160]{0:T(256)S(1)}, s32[160]{0:T(256)S(1)}, u32[]{:S(2)}, u32[]{:S(2)}) %collective-permute-start.1) | collective-permute-done | bytes 672 | tf_op jit(solution)/shard_map/while/body/eval_jaxpr/ppermute | solution.py:13
  144.3 1.9 collective-permute-start
  146.2 1.9 collective-permute-start.2
  150.1 7.9 %collective-permute-done.1 = s32[160]{0:T(256)S(1)} collective-permute-done((s32[160]{0:T(256)S(1)}, s32[160]{0:T(256)S(1)}, u32[]{:S(2)}, u32[]{:S(2)}) %collective-permute-start.1) | collective-permute-done | bytes 672 | tf_op jit(solution)/shard_map/while/body/eval_jaxpr/ppermute | solution.py:13
  158.8 1.9 collective-permute-start
  160.8 1.9 collective-permute-start.2
  162.7 1.9 collective-permute-start.1
  164.6 7.1 %collective-permute-done.1 = s32[160]{0:T(256)S(1)} collective-permute-done((s32[160]{0:T(256)S(1)}, s32[160]{0:T(256)S(1)}, u32[]{:S(2)}, u32[]{:S(2)}) %collective-permute-start.1) | collective-permute-done | bytes 672 | tf_op jit(solution)/shard_map/while/body/eval_jaxpr/ppermute | solution.py:13
  178.3 7.1 %collective-permute-done.1 = s32[160]{0:T(256)S(1)} collective-permute-done((s32[160]{0:T(256)S(1)}, s32[160]{0:T(256)S(1)}, u32[]{:S(2)}, u32[]{:S(2)}) %collective-permute-start.1) | collective-permute-done | bytes 672 | tf_op jit(solution)/shard_map/while/body/eval_jaxpr/ppermute | solution.py:13
  190.1 2.5 collective-permute-start.1
  192.7 6.9 %collective-permute-done.1 = s32[160]{0:T(256)S(1)} collective-permute-done((s32[160]{0:T(256)S(1)}, s32[160]{0:T(256)S(1)}, u32[]{:S(2)}, u32[]{:S(2)}) %collective-permute-start.1) | collective-permute-done | bytes 672 | tf_op jit(solution)/shard_map/while/body/eval_jaxpr/ppermute | solution.py:13
  204.2 4.0 collective-permute-start.1
  208.2 6.5 %collective-permute-done.1 = s32[160]{0:T(256)S(1)} collective-permute-done((s32[160]{0:T(256)S(1)}, s32[160]{0:T(256)S(1)}, u32[]{:S(2)}, u32[]{:S(2)}) %collective-permute-start.1) | collective-permute-done | bytes 672 | tf_op jit(solution)/shard_map/while/body/eval_jaxpr/ppermute | solution.py:13
  217.5 2.3 collective-permute-start.2
  219.8 3.0 collective-permute-start.1
  222.8 8.2 %collective-permute-done.1 = s32[160]{0:T(256)S(1)} collective-permute-done((s32[160]{0:T(256)S(1)}, s32[160]{0:T(256)S(1)}, u32[]{:S(2)}, u32[]{:S(2)}) %collective-permute-start.1) | collective-permute-done | bytes 672 | tf_op jit(solution)/shard_map/while/body/eval_jaxpr/ppermute | solution.py:13
  233.7 2.3 collective-permute-start.2
  236.0 2.4 collective-permute-start.1
  238.5 10.4 %collective-permute-done.1 = s32[160]{0:T(256)S(1)} collective-permute-done((s32[160]{0:T(256)S(1)}, s32[160]{0:T(256)S(1)}, u32[]{:S(2)}, u32[]{:S(2)}) %collective-permute-start.1) | collective-permute-done | bytes 672 | tf_op jit(solution)/shard_map/while/body/eval_jaxpr/ppermute | solution.py:13
  255.5 12.1 %collective-permute-done.1 = s32[160]{0:T(256)S(1)} collective-permute-done((s32[160]{0:T(256)S(1)}, s32[160]{0:T(256)S(1)}, u32[]{:S(2)}, u32[]{:S(2)}) %collective-permute-start.1) | collective-permute-done | bytes 672 | tf_op jit(solution)/shard_map/while/body/eval_jaxpr/ppermute | solution.py:13
  274.2 11.5 %collective-permute-done.1 = s32[160]{0:T(256)S(1)} collective-permute-done((s32[160]{0:T(256)S(1)}, s32[160]{0:T(256)S(1)}, u32[]{:S(2)}, u32[]{:S(2)}) %collective-permute-start.1) | collective-permute-done | bytes 672 | tf_op jit(solution)/shard_map/while/body/eval_jaxpr/ppermute | solution.py:13
  292.3 10.6 %collective-permute-done.1 = s32[160]{0:T(256)S(1)} collective-permute-done((s32[160]{0:T(256)S(1)}, s32[160]{0:T(256)S(1)}, u32[]{:S(2)}, u32[]{:S(2)}) %collective-permute-start.1) | collective-permute-done | bytes 672 | tf_op jit(solution)/shard_map/while/body/eval_jaxpr/ppermute | solution.py:13
  303.7 1.9 collective-permute-start
  305.7 1.9 collective-permute-start.2
  307.6 1.9 collective-permute-start.1
  309.5 9.7 %collective-permute-done.1 = s32[160]{0:T(256)S(1)} collective-permute-done((s32[160]{0:T(256)S(1)}, s32[160]{0:T(256)S(1)}, u32[]{:S(2)}, u32[]{:S(2)}) %collective-permute-start.1) | collective-permute-done | bytes 672 | tf_op jit(solution)/shard_map/while/body/eval_jaxpr/ppermute | solution.py:13
  322.6 2.1 collective-permute-start.3
  326.1 6.8 %collective-permute-done.3 = bf16[160,768]{1,0:T(8,128)(2,1)S(1)} collective-permute-done((bf16[160,768]{1,0:T(8,128)(2,1)S(1)}, bf16[160,768]{1,0:T(8,128)(2,1)S(1)}, u32[]{:S(2)}, u32[]{:S(2)}) %collective-permute-start.3) | collective-permute-done | bytes 245792 | tf_op jit(solution)/shard_map/ppermute | solution.py:13
  334.0 81.0 %reduce-scatter.4.cloned.1.call-done = bf16[32,768]{1,0:T(8,128)(2,1)} async-done(((bf16[1024,768]{1,0:T(8,128)(2,1)}), bf16[32,768]{1,0:T(8,128)(2,1)}) %reduce-scatter.4.cloned.1.call-update) | async-done | bytes 49168
  416.0 64.6 %psum.7 = bf16[32,768]{0,1:T(8,128)(2,1)S(1)} all-reduce(bf16[32,768]{0,1:T(8,128)(2,1)S(1)} %copy.10), channel_id=1, replica_groups=mesh['blk'=16,'group'=32] {'blk'}, use_global_device_ids=true, to_apply=%region_7.0 | all-reduce | flops 24576 | bytes 98304 | tf_op jit(solution)/shard_map/psum | solution.py:84
  (153 shorter events, 59.5 us)
Async XLA Ops:
  7.2 66.6 %all-gather.2.cloned.1.call-start = ((), (), s32[]{:S(2)}) async-start(), calls=%async_computation.1 | async-start | bytes 1622016 | tf_op jit(solution)/shard_map/all_gather | solution.py:46
  7.9 407.1 %reduce-scatter.4.cloned.1.call-start = ((), (), s32[]{:S(2)}) async-start(), calls=%async_computation.2 | async-start | bytes 1622016
  76.6 17.5 %collective-permute-start = (bf16[160,768]{1,0:T(8,128)(2,1)S(1)}, bf16[160,768]{1,0:T(8,128)(2,1)S(1)}, u32[]{:S(2)}, u32[]{:S(2)}) collective-permute-start(bf16[160,768]{1,0:T(8,128)(2,1)S(1)} %get-tuple-element.117), channel_id=1, source_target_pairs={{480,0},{0,32},{32,64},{64,96},{96,128},{128,160},{160,192},{192,2... | collective-permute-start | bytes 737288 | tf_op jit(solution)/shard_map/while/body/eval_jaxpr/ppermute | solution.py:13
  80.0 14.4 %collective-permute-start.2 = (bf16[160,768]{1,0:T(8,128)(2,1)S(1)}, bf16[160,768]{1,0:T(8,128)(2,1)S(1)}, u32[]{:S(2)}, u32[]{:S(2)}) collective-permute-start(bf16[160,768]{1,0:T(8,128)(2,1)S(1)} %get-tuple-element.119), channel_id=1, source_target_pairs={{480,0},{0,32},{32,64},{64,96},{96,128},{128,160},{160,192},{192,2... | collective-permute-start | bytes 737288 | tf_op jit(solution)/shard_map/while/body/eval_jaxpr/ppermute | solution.py:13
  83.4 10.7 %collective-permute-start.1 = (s32[160]{0:T(256)S(1)}, s32[160]{0:T(256)S(1)}, u32[]{:S(2)}, u32[]{:S(2)}) collective-permute-start(s32[160]{0:T(256)S(1)} %get-tuple-element.118), channel_id=1, source_target_pairs={{480,0},{0,32},{32,64},{64,96},{96,128},{128,160},{160,192},{192,2... | collective-permute-start | bytes 1928 | tf_op jit(solution)/shard_map/while/body/eval_jaxpr/ppermute | solution.py:13
  94.9 16.6 %collective-permute-start = (bf16[160,768]{1,0:T(8,128)(2,1)S(1)}, bf16[160,768]{1,0:T(8,128)(2,1)S(1)}, u32[]{:S(2)}, u32[]{:S(2)}) collective-permute-start(bf16[160,768]{1,0:T(8,128)(2,1)S(1)} %get-tuple-element.117), channel_id=1, source_target_pairs={{480,0},{0,32},{32,64},{64,96},{96,128},{128,160},{160,192},{192,2... | collective-permute-start | bytes 737288 | tf_op jit(solution)/shard_map/while/body/eval_jaxpr/ppermute | solution.py:13
  96.8 15.0 %collective-permute-start.2 = (bf16[160,768]{1,0:T(8,128)(2,1)S(1)}, bf16[160,768]{1,0:T(8,128)(2,1)S(1)}, u32[]{:S(2)}, u32[]{:S(2)}) collective-permute-start(bf16[160,768]{1,0:T(8,128)(2,1)S(1)} %get-tuple-element.119), channel_id=1, source_target_pairs={{480,0},{0,32},{32,64},{64,96},{96,128},{128,160},{160,192},{192,2... | collective-permute-start | bytes 737288 | tf_op jit(solution)/shard_map/while/body/eval_jaxpr/ppermute | solution.py:13
  99.6 11.9 %collective-permute-start.1 = (s32[160]{0:T(256)S(1)}, s32[160]{0:T(256)S(1)}, u32[]{:S(2)}, u32[]{:S(2)}) collective-permute-start(s32[160]{0:T(256)S(1)} %get-tuple-element.118), channel_id=1, source_target_pairs={{480,0},{0,32},{32,64},{64,96},{96,128},{128,160},{160,192},{192,2... | collective-permute-start | bytes 1928 | tf_op jit(solution)/shard_map/while/body/eval_jaxpr/ppermute | solution.py:13
  112.3 15.7 %collective-permute-start = (bf16[160,768]{1,0:T(8,128)(2,1)S(1)}, bf16[160,768]{1,0:T(8,128)(2,1)S(1)}, u32[]{:S(2)}, u32[]{:S(2)}) collective-permute-start(bf16[160,768]{1,0:T(8,128)(2,1)S(1)} %get-tuple-element.117), channel_id=1, source_target_pairs={{480,0},{0,32},{32,64},{64,96},{96,128},{128,160},{160,192},{192,2... | collective-permute-start | bytes 737288 | tf_op jit(solution)/shard_map/while/body/eval_jaxpr/ppermute | solution.py:13
  114.3 14.0 %collective-permute-start.2 = (bf16[160,768]{1,0:T(8,128)(2,1)S(1)}, bf16[160,768]{1,0:T(8,128)(2,1)S(1)}, u32[]{:S(2)}, u32[]{:S(2)}) collective-permute-start(bf16[160,768]{1,0:T(8,128)(2,1)S(1)} %get-tuple-element.119), channel_id=1, source_target_pairs={{480,0},{0,32},{32,64},{64,96},{96,128},{128,160},{160,192},{192,2... | collective-permute-start | bytes 737288 | tf_op jit(solution)/shard_map/while/body/eval_jaxpr/ppermute | solution.py:13
  116.2 11.8 %collective-permute-start.1 = (s32[160]{0:T(256)S(1)}, s32[160]{0:T(256)S(1)}, u32[]{:S(2)}, u32[]{:S(2)}) collective-permute-start(s32[160]{0:T(256)S(1)} %get-tuple-element.118), channel_id=1, source_target_pairs={{480,0},{0,32},{32,64},{64,96},{96,128},{128,160},{160,192},{192,2... | collective-permute-start | bytes 1928 | tf_op jit(solution)/shard_map/while/body/eval_jaxpr/ppermute | solution.py:13
  128.8 14.7 %collective-permute-start = (bf16[160,768]{1,0:T(8,128)(2,1)S(1)}, bf16[160,768]{1,0:T(8,128)(2,1)S(1)}, u32[]{:S(2)}, u32[]{:S(2)}) collective-permute-start(bf16[160,768]{1,0:T(8,128)(2,1)S(1)} %get-tuple-element.117), channel_id=1, source_target_pairs={{480,0},{0,32},{32,64},{64,96},{96,128},{128,160},{160,192},{192,2... | collective-permute-start | bytes 737288 | tf_op jit(solution)/shard_map/while/body/eval_jaxpr/ppermute | solution.py:13
  130.8 13.0 %collective-permute-start.2 = (bf16[160,768]{1,0:T(8,128)(2,1)S(1)}, bf16[160,768]{1,0:T(8,128)(2,1)S(1)}, u32[]{:S(2)}, u32[]{:S(2)}) collective-permute-start(bf16[160,768]{1,0:T(8,128)(2,1)S(1)} %get-tuple-element.119), channel_id=1, source_target_pairs={{480,0},{0,32},{32,64},{64,96},{96,128},{128,160},{160,192},{192,2... | collective-permute-start | bytes 737288 | tf_op jit(solution)/shard_map/while/body/eval_jaxpr/ppermute | solution.py:13
  132.7 10.8 %collective-permute-start.1 = (s32[160]{0:T(256)S(1)}, s32[160]{0:T(256)S(1)}, u32[]{:S(2)}, u32[]{:S(2)}) collective-permute-start(s32[160]{0:T(256)S(1)} %get-tuple-element.118), channel_id=1, source_target_pairs={{480,0},{0,32},{32,64},{64,96},{96,128},{128,160},{160,192},{192,2... | collective-permute-start | bytes 1928 | tf_op jit(solution)/shard_map/while/body/eval_jaxpr/ppermute | solution.py:13
  144.3 13.7 %collective-permute-start = (bf16[160,768]{1,0:T(8,128)(2,1)S(1)}, bf16[160,768]{1,0:T(8,128)(2,1)S(1)}, u32[]{:S(2)}, u32[]{:S(2)}) collective-permute-start(bf16[160,768]{1,0:T(8,128)(2,1)S(1)} %get-tuple-element.117), channel_id=1, source_target_pairs={{480,0},{0,32},{32,64},{64,96},{96,128},{128,160},{160,192},{192,2... | collective-permute-start | bytes 737288 | tf_op jit(solution)/shard_map/while/body/eval_jaxpr/ppermute | solution.py:13
  146.2 12.1 %collective-permute-start.2 = (bf16[160,768]{1,0:T(8,128)(2,1)S(1)}, bf16[160,768]{1,0:T(8,128)(2,1)S(1)}, u32[]{:S(2)}, u32[]{:S(2)}) collective-permute-start(bf16[160,768]{1,0:T(8,128)(2,1)S(1)} %get-tuple-element.119), channel_id=1, source_target_pairs={{480,0},{0,32},{32,64},{64,96},{96,128},{128,160},{160,192},{192,2... | collective-permute-start | bytes 737288 | tf_op jit(solution)/shard_map/while/body/eval_jaxpr/ppermute | solution.py:13
  148.2 9.8 %collective-permute-start.1 = (s32[160]{0:T(256)S(1)}, s32[160]{0:T(256)S(1)}, u32[]{:S(2)}, u32[]{:S(2)}) collective-permute-start(s32[160]{0:T(256)S(1)} %get-tuple-element.118), channel_id=1, source_target_pairs={{480,0},{0,32},{32,64},{64,96},{96,128},{128,160},{160,192},{192,2... | collective-permute-start | bytes 1928 | tf_op jit(solution)/shard_map/while/body/eval_jaxpr/ppermute | solution.py:13
  158.8 12.9 %collective-permute-start = (bf16[160,768]{1,0:T(8,128)(2,1)S(1)}, bf16[160,768]{1,0:T(8,128)(2,1)S(1)}, u32[]{:S(2)}, u32[]{:S(2)}) collective-permute-start(bf16[160,768]{1,0:T(8,128)(2,1)S(1)} %get-tuple-element.117), channel_id=1, source_target_pairs={{480,0},{0,32},{32,64},{64,96},{96,128},{128,160},{160,192},{192,2... | collective-permute-start | bytes 737288 | tf_op jit(solution)/shard_map/while/body/eval_jaxpr/ppermute | solution.py:13
  160.8 11.3 %collective-permute-start.2 = (bf16[160,768]{1,0:T(8,128)(2,1)S(1)}, bf16[160,768]{1,0:T(8,128)(2,1)S(1)}, u32[]{:S(2)}, u32[]{:S(2)}) collective-permute-start(bf16[160,768]{1,0:T(8,128)(2,1)S(1)} %get-tuple-element.119), channel_id=1, source_target_pairs={{480,0},{0,32},{32,64},{64,96},{96,128},{128,160},{160,192},{192,2... | collective-permute-start | bytes 737288 | tf_op jit(solution)/shard_map/while/body/eval_jaxpr/ppermute | solution.py:13
  162.7 9.0 %collective-permute-start.1 = (s32[160]{0:T(256)S(1)}, s32[160]{0:T(256)S(1)}, u32[]{:S(2)}, u32[]{:S(2)}) collective-permute-start(s32[160]{0:T(256)S(1)} %get-tuple-element.118), channel_id=1, source_target_pairs={{480,0},{0,32},{32,64},{64,96},{96,128},{128,160},{160,192},{192,2... | collective-permute-start | bytes 1928 | tf_op jit(solution)/shard_map/while/body/eval_jaxpr/ppermute | solution.py:13
  172.6 12.9 %collective-permute-start = (bf16[160,768]{1,0:T(8,128)(2,1)S(1)}, bf16[160,768]{1,0:T(8,128)(2,1)S(1)}, u32[]{:S(2)}, u32[]{:S(2)}) collective-permute-start(bf16[160,768]{1,0:T(8,128)(2,1)S(1)} %get-tuple-element.117), channel_id=1, source_target_pairs={{480,0},{0,32},{32,64},{64,96},{96,128},{128,160},{160,192},{192,2... | collective-permute-start | bytes 737288 | tf_op jit(solution)/shard_map/while/body/eval_jaxpr/ppermute | solution.py:13
  174.5 11.3 %collective-permute-start.2 = (bf16[160,768]{1,0:T(8,128)(2,1)S(1)}, bf16[160,768]{1,0:T(8,128)(2,1)S(1)}, u32[]{:S(2)}, u32[]{:S(2)}) collective-permute-start(bf16[160,768]{1,0:T(8,128)(2,1)S(1)} %get-tuple-element.119), channel_id=1, source_target_pairs={{480,0},{0,32},{32,64},{64,96},{96,128},{128,160},{160,192},{192,2... | collective-permute-start | bytes 737288 | tf_op jit(solution)/shard_map/while/body/eval_jaxpr/ppermute | solution.py:13
  176.4 9.0 %collective-permute-start.1 = (s32[160]{0:T(256)S(1)}, s32[160]{0:T(256)S(1)}, u32[]{:S(2)}, u32[]{:S(2)}) collective-permute-start(s32[160]{0:T(256)S(1)} %get-tuple-element.118), channel_id=1, source_target_pairs={{480,0},{0,32},{32,64},{64,96},{96,128},{128,160},{160,192},{192,2... | collective-permute-start | bytes 1928 | tf_op jit(solution)/shard_map/while/body/eval_jaxpr/ppermute | solution.py:13
  186.3 13.3 %collective-permute-start = (bf16[160,768]{1,0:T(8,128)(2,1)S(1)}, bf16[160,768]{1,0:T(8,128)(2,1)S(1)}, u32[]{:S(2)}, u32[]{:S(2)}) collective-permute-start(bf16[160,768]{1,0:T(8,128)(2,1)S(1)} %get-tuple-element.117), channel_id=1, source_target_pairs={{480,0},{0,32},{32,64},{64,96},{96,128},{128,160},{160,192},{192,2... | collective-permute-start | bytes 737288 | tf_op jit(solution)/shard_map/while/body/eval_jaxpr/ppermute | solution.py:13
  188.2 11.7 %collective-permute-start.2 = (bf16[160,768]{1,0:T(8,128)(2,1)S(1)}, bf16[160,768]{1,0:T(8,128)(2,1)S(1)}, u32[]{:S(2)}, u32[]{:S(2)}) collective-permute-start(bf16[160,768]{1,0:T(8,128)(2,1)S(1)} %get-tuple-element.119), channel_id=1, source_target_pairs={{480,0},{0,32},{32,64},{64,96},{96,128},{128,160},{160,192},{192,2... | collective-permute-start | bytes 737288 | tf_op jit(solution)/shard_map/while/body/eval_jaxpr/ppermute | solution.py:13
  190.1 9.4 %collective-permute-start.1 = (s32[160]{0:T(256)S(1)}, s32[160]{0:T(256)S(1)}, u32[]{:S(2)}, u32[]{:S(2)}) collective-permute-start(s32[160]{0:T(256)S(1)} %get-tuple-element.118), channel_id=1, source_target_pairs={{480,0},{0,32},{32,64},{64,96},{96,128},{128,160},{160,192},{192,2... | collective-permute-start | bytes 1928 | tf_op jit(solution)/shard_map/while/body/eval_jaxpr/ppermute | solution.py:13
  200.4 14.4 %collective-permute-start = (bf16[160,768]{1,0:T(8,128)(2,1)S(1)}, bf16[160,768]{1,0:T(8,128)(2,1)S(1)}, u32[]{:S(2)}, u32[]{:S(2)}) collective-permute-start(bf16[160,768]{1,0:T(8,128)(2,1)S(1)} %get-tuple-element.117), channel_id=1, source_target_pairs={{480,0},{0,32},{32,64},{64,96},{96,128},{128,160},{160,192},{192,2... | collective-permute-start | bytes 737288 | tf_op jit(solution)/shard_map/while/body/eval_jaxpr/ppermute | solution.py:13
  202.3 12.7 %collective-permute-start.2 = (bf16[160,768]{1,0:T(8,128)(2,1)S(1)}, bf16[160,768]{1,0:T(8,128)(2,1)S(1)}, u32[]{:S(2)}, u32[]{:S(2)}) collective-permute-start(bf16[160,768]{1,0:T(8,128)(2,1)S(1)} %get-tuple-element.119), channel_id=1, source_target_pairs={{480,0},{0,32},{32,64},{64,96},{96,128},{128,160},{160,192},{192,2... | collective-permute-start | bytes 737288 | tf_op jit(solution)/shard_map/while/body/eval_jaxpr/ppermute | solution.py:13
  204.2 10.5 %collective-permute-start.1 = (s32[160]{0:T(256)S(1)}, s32[160]{0:T(256)S(1)}, u32[]{:S(2)}, u32[]{:S(2)}) collective-permute-start(s32[160]{0:T(256)S(1)} %get-tuple-element.118), channel_id=1, source_target_pairs={{480,0},{0,32},{32,64},{64,96},{96,128},{128,160},{160,192},{192,2... | collective-permute-start | bytes 1928 | tf_op jit(solution)/shard_map/while/body/eval_jaxpr/ppermute | solution.py:13
  215.6 15.4 %collective-permute-start = (bf16[160,768]{1,0:T(8,128)(2,1)S(1)}, bf16[160,768]{1,0:T(8,128)(2,1)S(1)}, u32[]{:S(2)}, u32[]{:S(2)}) collective-permute-start(bf16[160,768]{1,0:T(8,128)(2,1)S(1)} %get-tuple-element.117), channel_id=1, source_target_pairs={{480,0},{0,32},{32,64},{64,96},{96,128},{128,160},{160,192},{192,2... | collective-permute-start | bytes 737288 | tf_op jit(solution)/shard_map/while/body/eval_jaxpr/ppermute | solution.py:13
  217.5 13.8 %collective-permute-start.2 = (bf16[160,768]{1,0:T(8,128)(2,1)S(1)}, bf16[160,768]{1,0:T(8,128)(2,1)S(1)}, u32[]{:S(2)}, u32[]{:S(2)}) collective-permute-start(bf16[160,768]{1,0:T(8,128)(2,1)S(1)} %get-tuple-element.119), channel_id=1, source_target_pairs={{480,0},{0,32},{32,64},{64,96},{96,128},{128,160},{160,192},{192,2... | collective-permute-start | bytes 737288 | tf_op jit(solution)/shard_map/while/body/eval_jaxpr/ppermute | solution.py:13
  219.8 11.2 %collective-permute-start.1 = (s32[160]{0:T(256)S(1)}, s32[160]{0:T(256)S(1)}, u32[]{:S(2)}, u32[]{:S(2)}) collective-permute-start(s32[160]{0:T(256)S(1)} %get-tuple-element.118), channel_id=1, source_target_pairs={{480,0},{0,32},{32,64},{64,96},{96,128},{128,160},{160,192},{192,2... | collective-permute-start | bytes 1928 | tf_op jit(solution)/shard_map/while/body/eval_jaxpr/ppermute | solution.py:13
  231.8 17.0 %collective-permute-start = (bf16[160,768]{1,0:T(8,128)(2,1)S(1)}, bf16[160,768]{1,0:T(8,128)(2,1)S(1)}, u32[]{:S(2)}, u32[]{:S(2)}) collective-permute-start(bf16[160,768]{1,0:T(8,128)(2,1)S(1)} %get-tuple-element.117), channel_id=1, source_target_pairs={{480,0},{0,32},{32,64},{64,96},{96,128},{128,160},{160,192},{192,2... | collective-permute-start | bytes 737288 | tf_op jit(solution)/shard_map/while/body/eval_jaxpr/ppermute | solution.py:13
  233.7 15.4 %collective-permute-start.2 = (bf16[160,768]{1,0:T(8,128)(2,1)S(1)}, bf16[160,768]{1,0:T(8,128)(2,1)S(1)}, u32[]{:S(2)}, u32[]{:S(2)}) collective-permute-start(bf16[160,768]{1,0:T(8,128)(2,1)S(1)} %get-tuple-element.119), channel_id=1, source_target_pairs={{480,0},{0,32},{32,64},{64,96},{96,128},{128,160},{160,192},{192,2... | collective-permute-start | bytes 737288 | tf_op jit(solution)/shard_map/while/body/eval_jaxpr/ppermute | solution.py:13
  236.0 12.8 %collective-permute-start.1 = (s32[160]{0:T(256)S(1)}, s32[160]{0:T(256)S(1)}, u32[]{:S(2)}, u32[]{:S(2)}) collective-permute-start(s32[160]{0:T(256)S(1)} %get-tuple-element.118), channel_id=1, source_target_pairs={{480,0},{0,32},{32,64},{64,96},{96,128},{128,160},{160,192},{192,2... | collective-permute-start | bytes 1928 | tf_op jit(solution)/shard_map/while/body/eval_jaxpr/ppermute | solution.py:13
  249.7 17.9 %collective-permute-start = (bf16[160,768]{1,0:T(8,128)(2,1)S(1)}, bf16[160,768]{1,0:T(8,128)(2,1)S(1)}, u32[]{:S(2)}, u32[]{:S(2)}) collective-permute-start(bf16[160,768]{1,0:T(8,128)(2,1)S(1)} %get-tuple-element.117), channel_id=1, source_target_pairs={{480,0},{0,32},{32,64},{64,96},{96,128},{128,160},{160,192},{192,2... | collective-permute-start | bytes 737288 | tf_op jit(solution)/shard_map/while/body/eval_jaxpr/ppermute | solution.py:13
  251.6 16.3 %collective-permute-start.2 = (bf16[160,768]{1,0:T(8,128)(2,1)S(1)}, bf16[160,768]{1,0:T(8,128)(2,1)S(1)}, u32[]{:S(2)}, u32[]{:S(2)}) collective-permute-start(bf16[160,768]{1,0:T(8,128)(2,1)S(1)} %get-tuple-element.119), channel_id=1, source_target_pairs={{480,0},{0,32},{32,64},{64,96},{96,128},{128,160},{160,192},{192,2... | collective-permute-start | bytes 737288 | tf_op jit(solution)/shard_map/while/body/eval_jaxpr/ppermute | solution.py:13
  253.5 14.1 %collective-permute-start.1 = (s32[160]{0:T(256)S(1)}, s32[160]{0:T(256)S(1)}, u32[]{:S(2)}, u32[]{:S(2)}) collective-permute-start(s32[160]{0:T(256)S(1)} %get-tuple-element.118), channel_id=1, source_target_pairs={{480,0},{0,32},{32,64},{64,96},{96,128},{128,160},{160,192},{192,2... | collective-permute-start | bytes 1928 | tf_op jit(solution)/shard_map/while/body/eval_jaxpr/ppermute | solution.py:13
  268.4 17.3 %collective-permute-start = (bf16[160,768]{1,0:T(8,128)(2,1)S(1)}, bf16[160,768]{1,0:T(8,128)(2,1)S(1)}, u32[]{:S(2)}, u32[]{:S(2)}) collective-permute-start(bf16[160,768]{1,0:T(8,128)(2,1)S(1)} %get-tuple-element.117), channel_id=1, source_target_pairs={{480,0},{0,32},{32,64},{64,96},{96,128},{128,160},{160,192},{192,2... | collective-permute-start | bytes 737288 | tf_op jit(solution)/shard_map/while/body/eval_jaxpr/ppermute | solution.py:13
  270.4 15.6 %collective-permute-start.2 = (bf16[160,768]{1,0:T(8,128)(2,1)S(1)}, bf16[160,768]{1,0:T(8,128)(2,1)S(1)}, u32[]{:S(2)}, u32[]{:S(2)}) collective-permute-start(bf16[160,768]{1,0:T(8,128)(2,1)S(1)} %get-tuple-element.119), channel_id=1, source_target_pairs={{480,0},{0,32},{32,64},{64,96},{96,128},{128,160},{160,192},{192,2... | collective-permute-start | bytes 737288 | tf_op jit(solution)/shard_map/while/body/eval_jaxpr/ppermute | solution.py:13
  272.3 13.4 %collective-permute-start.1 = (s32[160]{0:T(256)S(1)}, s32[160]{0:T(256)S(1)}, u32[]{:S(2)}, u32[]{:S(2)}) collective-permute-start(s32[160]{0:T(256)S(1)} %get-tuple-element.118), channel_id=1, source_target_pairs={{480,0},{0,32},{32,64},{64,96},{96,128},{128,160},{160,192},{192,2... | collective-permute-start | bytes 1928 | tf_op jit(solution)/shard_map/while/body/eval_jaxpr/ppermute | solution.py:13
  286.5 16.4 %collective-permute-start = (bf16[160,768]{1,0:T(8,128)(2,1)S(1)}, bf16[160,768]{1,0:T(8,128)(2,1)S(1)}, u32[]{:S(2)}, u32[]{:S(2)}) collective-permute-start(bf16[160,768]{1,0:T(8,128)(2,1)S(1)} %get-tuple-element.117), channel_id=1, source_target_pairs={{480,0},{0,32},{32,64},{64,96},{96,128},{128,160},{160,192},{192,2... | collective-permute-start | bytes 737288 | tf_op jit(solution)/shard_map/while/body/eval_jaxpr/ppermute | solution.py:13
  288.5 14.8 %collective-permute-start.2 = (bf16[160,768]{1,0:T(8,128)(2,1)S(1)}, bf16[160,768]{1,0:T(8,128)(2,1)S(1)}, u32[]{:S(2)}, u32[]{:S(2)}) collective-permute-start(bf16[160,768]{1,0:T(8,128)(2,1)S(1)} %get-tuple-element.119), channel_id=1, source_target_pairs={{480,0},{0,32},{32,64},{64,96},{96,128},{128,160},{160,192},{192,2... | collective-permute-start | bytes 737288 | tf_op jit(solution)/shard_map/while/body/eval_jaxpr/ppermute | solution.py:13
  290.4 12.5 %collective-permute-start.1 = (s32[160]{0:T(256)S(1)}, s32[160]{0:T(256)S(1)}, u32[]{:S(2)}, u32[]{:S(2)}) collective-permute-start(s32[160]{0:T(256)S(1)} %get-tuple-element.118), channel_id=1, source_target_pairs={{480,0},{0,32},{32,64},{64,96},{96,128},{128,160},{160,192},{192,2... | collective-permute-start | bytes 1928 | tf_op jit(solution)/shard_map/while/body/eval_jaxpr/ppermute | solution.py:13
  303.7 15.5 %collective-permute-start = (bf16[160,768]{1,0:T(8,128)(2,1)S(1)}, bf16[160,768]{1,0:T(8,128)(2,1)S(1)}, u32[]{:S(2)}, u32[]{:S(2)}) collective-permute-start(bf16[160,768]{1,0:T(8,128)(2,1)S(1)} %get-tuple-element.117), channel_id=1, source_target_pairs={{480,0},{0,32},{32,64},{64,96},{96,128},{128,160},{160,192},{192,2... | collective-permute-start | bytes 737288 | tf_op jit(solution)/shard_map/while/body/eval_jaxpr/ppermute | solution.py:13
  305.7 13.8 %collective-permute-start.2 = (bf16[160,768]{1,0:T(8,128)(2,1)S(1)}, bf16[160,768]{1,0:T(8,128)(2,1)S(1)}, u32[]{:S(2)}, u32[]{:S(2)}) collective-permute-start(bf16[160,768]{1,0:T(8,128)(2,1)S(1)} %get-tuple-element.119), channel_id=1, source_target_pairs={{480,0},{0,32},{32,64},{64,96},{96,128},{128,160},{160,192},{192,2... | collective-permute-start | bytes 737288 | tf_op jit(solution)/shard_map/while/body/eval_jaxpr/ppermute | solution.py:13
  307.6 11.6 %collective-permute-start.1 = (s32[160]{0:T(256)S(1)}, s32[160]{0:T(256)S(1)}, u32[]{:S(2)}, u32[]{:S(2)}) collective-permute-start(s32[160]{0:T(256)S(1)} %get-tuple-element.118), channel_id=1, source_target_pairs={{480,0},{0,32},{32,64},{64,96},{96,128},{128,160},{160,192},{192,2... | collective-permute-start | bytes 1928 | tf_op jit(solution)/shard_map/while/body/eval_jaxpr/ppermute | solution.py:13
  322.6 10.3 %collective-permute-start.3 = (bf16[160,768]{1,0:T(8,128)(2,1)S(1)}, bf16[160,768]{1,0:T(8,128)(2,1)S(1)}, u32[]{:S(2)}, u32[]{:S(2)}) collective-permute-start(bf16[160,768]{1,0:T(8,128)(2,1)S(1)} %get-tuple-element.42), channel_id=1, source_target_pairs={{480,0},{0,32},{32,64},{64,96},{96,128},{128,160},{160,192},{192,2... | collective-permute-start | bytes 737288 | tf_op jit(solution)/shard_map/ppermute | solution.py:13
  (4 other events, 144.0 us)
Sparse Core Ops, SparseCore 0:
  11.1 62.5 all-gather.1
  322.7 92.3 reduce-scatter.3
where the time goes:
time: 490 us; the launch traced here: 488 us
  waiting for transfers between devices  281 us (57%)
  starting transfers between devices  103 us (21%)
  blocking collectives  64.6 us (13%)
  matrix products  16.2 us (3%)
  between operations  14.2 us (3%)
    ppermute x46, waiting for transfers between devices, shifted(): return lax.ppermute(block, axis, route)  137 us
    ppermute x46, starting transfers between devices, shifted(): return lax.ppermute(block, axis, route)  103 us
    unnamed x3, waiting for transfers between devices  81.7 us
    psum x1, blocking collectives, on_device(): weight_grad = lax.psum(weight_share, 'blk').astype(jnp.float32)  64.6 us
    all_gather x1, waiting for transfers between devices, on_device(): lax.all_gather(audio_weight, 'group', axis=0, tiled=True)  62.9 us
  transfers between devices with their start and end apart: 48, of which 18 were waited for; matrix products, arithmetic and copies ran while one was open for 2% of the time, Pallas kernels for 0%

commit v1 on v0

v1 whole, which is shorter than its diff:
```python
import jax
import jax.numpy as jnp
from jax import lax
from jax.experimental import pallas as pl
from jax.experimental.pallas import tpu as pltpu
from jax.sharding import PartitionSpec as P

MESH = pl.DeviceIdType.MESH
BF = jnp.bfloat16
F32 = jnp.float32
SCALE = 16.0
SHIFT = -4.0
EPS = 1e-6
ROWS, WIDE, COLS, HALF = 160, 1024, 768, 80


def kernel(
    audio_hbm, text_hbm, labels_ref, weight_hbm,
    audio_out, text_out, grad_out,
    audio, text, texts, label_rows, pair_label, weight, units, unit_low, norms, d_audio, d_text,
    dp_low, pair_dp, rs_out, rs_in, audio_res, text_res, grad_res,
    load_sem, store_sem, gs, gr, ls, lr, w1s, w1r, w2s, w2r, wcs, wcr, ps, pr, rss, rsr,
):
    blk, group = lax.axis_index("blk"), lax.axis_index("group")
    z_lo, y = blk // 8, blk % 8
    z_hi, x, core = group // 8, (group // 2) % 4, group % 2

    def at_y(step):
        return (z_lo * 8 + (y + step + 8) % 8, group)

    def at_x(step):
        return (blk, z_hi * 8 + ((x + step) % 4) * 2 + core)

    def at_z(step):
        return (blk, ((z_hi + step) % 4) * 8 + x * 2 + core)

    pair = ((1 - z_lo) * 8 + y, group)
    other = (blk, z_hi * 8 + x * 2 + (1 - core))
    ring = (at_y(1), at_y(-1))
    started = []

    def send(src, dst, s, r, to):
        copy = pltpu.make_async_remote_copy(
            src_ref=src, dst_ref=dst, send_sem=s, recv_sem=r, device_id=to, device_id_type=MESH
        )
        copy.start()
        started.append(copy)

    def arrived(dst, s, r):
        pltpu.make_async_remote_copy(
            src_ref=dst, dst_ref=dst, send_sem=s, recv_sem=r, device_id=ring[0], device_id_type=MESH
        ).wait_recv()

    loads = [
        pltpu.make_async_copy(text_hbm, text, load_sem.at[0]),
        pltpu.make_async_copy(weight_hbm, weight.at[z_hi, x * 2 + core], load_sem.at[1]),
        pltpu.make_async_copy(audio_hbm, audio.at[0], load_sem.at[2]),
    ]
    for load in loads:
        load.start()

    barrier = pltpu.get_barrier_semaphore()
    friends = ring + (pair, other) + tuple(at_z(i) for i in (1, 2, 3)) + tuple(at_x(i) for i in (1, 2, 3))
    for friend in friends:
        pl.semaphore_signal(barrier, inc=1, device_id=friend, device_id_type=MESH)

    loads[0].wait()
    raw = text[...].astype(F32)
    texts[0] = (raw / jnp.sqrt(jnp.sum(raw * raw, axis=-1, keepdims=True) + EPS)).astype(BF)
    label_rows[0] = jnp.broadcast_to(labels_ref[...].astype(F32), (8, ROWS))
    loads[1].wait()
    loads[2].wait()
    pl.semaphore_wait(barrier, len(friends))

    def part(k):
        return pl.ds(k * HALF, HALF)

    def slot_of(d, hop):
        return 2 * hop - 1 + d if hop < 4 else 7

    def gather_send(d, hop, k):
        src = 0 if hop == 1 else slot_of(d, hop - 1)
        send(
            texts.at[src, part(k)], texts.at[slot_of(d, hop), part(k)],
            gs.at[d, hop - 1, k], gr.at[d, hop - 1, k], ring[d],
        )

    def gather_wait(d, hop, k):
        arrived(texts.at[slot_of(d, hop), part(k)], gs.at[d, hop - 1, k], gr.at[d, hop - 1, k])

    def label_send(d, hop):
        src = 0 if hop == 1 else slot_of(d, hop - 1)
        send(
            label_rows.at[src], label_rows.at[slot_of(d, hop)],
            ls.at[d, hop - 1], lr.at[d, hop - 1], ring[d],
        )

    for k in (0, 1):
        for d in (0, 1):
            gather_send(d, 1, d if k == 0 else 1 - d)
    for d in (0, 1):
        label_send(d, 1)
    mine = weight.at[z_hi, x * 2 + core]
    for i in (1, 2, 3):
        send(mine, mine, w1s.at[i - 1], w1r.at[i - 1], at_z(i))
    send(label_rows.at[0], pair_label, ps.at[0], pr.at[0], pair)
    send(audio.at[0], audio.at[1], ps.at[1], pr.at[1], pair)

    def gather_hop(hop):
        for k in (0, 1):
            for d in (0, 1):
                which = d if k == 0 else 1 - d
                if hop == 4 and which != d:
                    continue
                gather_wait(d, hop, which)
                if hop < 3 or (hop == 3 and which == d):
                    gather_send(d, hop + 1, which)
        for d in (0, 1):
            if hop == 4 and d == 1:
                continue
            arrived(label_rows.at[slot_of(d, hop)], ls.at[d, hop - 1], lr.at[d, hop - 1])
            if hop < 3 or (hop == 3 and d == 0):
                label_send(d, hop + 1)

    gather_hop(1)
    for i in (1, 2, 3):
        there = weight.at[(z_hi + 4 - i) % 4, x * 2 + core]
        arrived(there, w1s.at[i - 1], w1r.at[i - 1])
    column = weight.at[:, x * 2 + core]
    for i in (1, 3, 2):
        send(column, column, w2s.at[i - 1], w2r.at[i - 1], at_x(i))
    send(column, column, wcs.at[0], wcr.at[0], other)
    gather_hop(2)
    for i in (1, 3, 2):
        there = weight.at[:, ((x + 4 - i) % 4) * 2 + core]
        arrived(there, w2s.at[i - 1], w2r.at[i - 1])
        send(there, there, wcs.at[i], wcr.at[i], other)
    gather_hop(3)
    for i in range(4):
        there = weight.at[:, ((x + 4 - i) % 4) * 2 + (1 - core)]
        arrived(there, wcs.at[i], wcr.at[i])
    arrived(pair_label, ps.at[0], pr.at[0])
    arrived(audio.at[1], ps.at[1], pr.at[1])

    whole = weight[...].reshape(WIDE, COLS)
    for i in (0, 1):
        proj = jnp.dot(audio[i], whole, preferred_element_type=F32)
        norm = jnp.sqrt(jnp.sum(proj * proj, axis=-1, keepdims=True) + EPS)
        unit = proj / norm
        units[i] = unit
        norms[i] = jnp.broadcast_to(norm, (ROWS, 128))
        unit_low[pl.ds(i * ROWS, ROWS)] = unit.astype(BF)

    diagonal = lax.broadcasted_iota(jnp.int32, (ROWS, ROWS), 0) == lax.broadcasted_iota(
        jnp.int32, (ROWS, ROWS), 1
    )

    def upright(row):
        return jnp.sum(jnp.where(diagonal, row, 0.0), axis=1, keepdims=True)

    own_labels = jnp.concatenate(
        [upright(label_rows[0][0:1, :]), upright(pair_label[...][0:1, :])], axis=0
    )

    d_audio[...] = jnp.zeros_like(d_audio)

    def block(slot):
        rows = texts[slot]
        logits = SCALE * lax.dot_general(
            unit_low[...], rows, (((1,), (1,)), ((), ())), preferred_element_type=F32
        ) + SHIFT
        positive = (own_labels == label_rows[slot][0:1, :]).astype(F32)
        pairs = (SCALE * (jax.nn.sigmoid(logits) - positive)).astype(BF)
        d_audio[...] += jnp.dot(pairs, rows, preferred_element_type=F32)
        d_text[slot] = lax.dot_general(
            pairs, unit_low[...], (((0,), (0,)), ((), ())), preferred_element_type=F32
        )

    def body(slot, carry):
        block(slot)
        return carry

    lax.fori_loop(0, 7, body, 0)

    def rs_send(d, r, k):
        slot = 7 if r == 4 else (2 * r if d == 0 else 2 * r - 1)
        value = d_text[slot, part(k), :]
        if r < 3 or (r == 3 and k == d):
            arrived(rs_in.at[d, r, part(k)], rss.at[d, r, k], rsr.at[d, r, k])
            value = value + rs_in[d, r, part(k), :].astype(F32)
        rs_out[d, r - 1, part(k), :] = value.astype(BF)
        send(
            rs_out.at[d, r - 1, part(k)], rs_in.at[d, r - 1, part(k)],
            rss.at[d, r - 1, k], rsr.at[d, r - 1, k], ring[d],
        )

    for d in (0, 1):
        rs_send(d, 3, 1 - d)
    gather_hop(4)
    block(7)
    for d in (0, 1):
        rs_send(d, 4, d)

    for i in (0, 1):
        total = d_audio[pl.ds(i * ROWS, ROWS), :]
        unit = units[i]
        share = (total - unit * jnp.sum(unit * total, axis=-1, keepdims=True)) / norms[i][:, 0:1]
        dp_low[pl.ds(i * ROWS, ROWS), :] = share.astype(BF)
        if i == 0:
            d_audio[pl.ds(0, ROWS), :] = share
    send(dp_low.at[pl.ds(ROWS, ROWS)], pair_dp, ps.at[2], pr.at[2], pair)

    for i in range(4):
        cut = pl.ds(i * 256, 256)
        grad_res[cut, :] = (
            lax.dot_general(audio[0, :, cut], dp_low[0:ROWS, :], (((0,), (0,)), ((), ())), preferred_element_type=F32)
            + lax.dot_general(audio[1, :, cut], dp_low[ROWS:, :], (((0,), (0,)), ((), ())), preferred_element_type=F32)
        ).astype(BF)
    store_grad = pltpu.make_async_copy(grad_res, grad_out, store_sem.at[2])
    store_grad.start()

    for d in (0, 1):
        rs_send(d, 3, d)
    for d in (0, 1):
        rs_send(d, 2, 1 - d)

    arrived(pair_dp, ps.at[2], pr.at[2])
    dproj = (d_audio[0:ROWS, :] + pair_dp[...].astype(F32)).astype(BF)
    audio_res[...] = lax.dot_general(
        dproj, weight[...].reshape(WIDE, COLS), (((1,), (1,)), ((), ())), preferred_element_type=F32
    ).astype(BF)
    store_audio = pltpu.make_async_copy(audio_res, audio_out, store_sem.at[0])
    store_audio.start()

    for d in (0, 1):
        rs_send(d, 2, d)
    for d in (0, 1):
        rs_send(d, 1, 1 - d)
    for d in (0, 1):
        rs_send(d, 1, d)
    for k in (0, 1):
        for d in (0, 1):
            arrived(rs_in.at[d, 0, part(k)], rss.at[d, 0, k], rsr.at[d, 0, k])
        total = d_text[0, part(k), :] + rs_in[0, 0, part(k), :].astype(F32) + rs_in[1, 0, part(k), :].astype(F32)
        raw = text[part(k), :].astype(F32)
        norm = jnp.sqrt(jnp.sum(raw * raw, axis=-1, keepdims=True) + EPS)
        unit = raw / norm
        text_res[part(k), :] = (
            (total - unit * jnp.sum(unit * total, axis=-1, keepdims=True)) / norm
        ).astype(BF)
    store_text = pltpu.make_async_copy(text_res, text_out, store_sem.at[1])
    store_text.start()
    for copy in started:
        copy.wait_send()
    store_grad.wait()
    store_audio.wait()
    store_text.wait()


def on_device(audio, text, labels, audio_weight):
    dma = pltpu.SemaphoreType.DMA
    audio_grad, text_grad, share = pl.pallas_call(
        kernel,
        out_shape=(
            jax.ShapeDtypeStruct((ROWS, WIDE), BF),
            jax.ShapeDtypeStruct((ROWS, COLS), BF),
            jax.ShapeDtypeStruct((WIDE, COLS), BF),
        ),
        in_specs=[
            pl.BlockSpec(memory_space=pl.ANY),
            pl.BlockSpec(memory_space=pl.ANY),
            pl.BlockSpec(memory_space=pltpu.VMEM),
            pl.BlockSpec(memory_space=pl.ANY),
        ],
        out_specs=[pl.BlockSpec(memory_space=pl.ANY)] * 3,
        scratch_shapes=[
            pltpu.VMEM((2, ROWS, WIDE), BF),
            pltpu.VMEM((ROWS, COLS), BF),
            pltpu.VMEM((8, ROWS, COLS), BF),
            pltpu.VMEM((8, 8, ROWS), F32),
            pltpu.VMEM((8, ROWS), F32),
            pltpu.VMEM((4, 8, 32, COLS), BF),
            pltpu.VMEM((2, ROWS, COLS), F32),
            pltpu.VMEM((2 * ROWS, COLS), BF),
            pltpu.VMEM((2, ROWS, 128), F32),
            pltpu.VMEM((2 * ROWS, COLS), F32),
            pltpu.VMEM((8, ROWS, COLS), F32),
            pltpu.VMEM((2 * ROWS, COLS), BF),
            pltpu.VMEM((ROWS, COLS), BF),
            pltpu.VMEM((2, 4, ROWS, COLS), BF),
            pltpu.VMEM((2, 4, ROWS, COLS), BF),
            pltpu.VMEM((ROWS, WIDE), BF),
            pltpu.VMEM((ROWS, COLS), BF),
            pltpu.VMEM((WIDE, COLS), BF),
            dma((3,)), dma((3,)),
            dma((2, 4, 2)), dma((2, 4, 2)),
            dma((2, 4)), dma((2, 4)),
            dma((3,)), dma((3,)),
            dma((3,)), dma((3,)),
            dma((4,)), dma((4,)),
            dma((3,)), dma((3,)),
            dma((2, 4, 2)), dma((2, 4, 2)),
        ],
        compiler_params=pltpu.CompilerParams(
            collective_id=0, has_side_effects=True, vmem_limit_bytes=48 * 2**20
        ),
    )(audio, text, labels.reshape(1, ROWS), audio_weight)
    grad = lax.psum_scatter(share, "group", scatter_dimension=0, tiled=True)
    weight_grad = lax.psum(grad, "blk").astype(F32)
    return (audio_grad, text_grad, weight_grad)


def solution(mesh):
    rows = P(("blk", "group"), None)
    return jax.shard_map(
        on_device,
        mesh=mesh,
        in_specs=(rows, rows, P(("blk", "group")), P("group", None)),
        out_specs=(rows, rows, P("group", None)),
        check_vma=False,
    )
```

time: 490 us -> 241 us (0.49)
  the two profiles are of different devices: /device:TPU:6 before, /device:TPU:2 now
where the time goes in v1:
time: 241 us; the launch traced here: 240 us
  waiting for transfers between devices  94.9 us (39%)
  blocking collectives  63.4 us (26%)
  Pallas kernels  62.6 us (26%)
  between operations  14 us (6%)
  local copies, waits for them, and re-layouts  4.8 us (2%)
    reduce_scatter x1, waiting for transfers between devices, on_device(): grad = lax.psum_scatter(share, 'group', scatter_dimension=0, tiled=True)  94.9 us
    psum x1, blocking collectives, on_device(): weight_grad = lax.psum(grad, 'blk').astype(F32)  63.4 us
    pallas_call x1, Pallas kernels, on_device(): pl.pallas_call(kernel, out_shape=(jax.ShapeDtypeStruct((ROWS, WIDE), BF),...  62.6 us
  transfers between devices with their start and end apart: 1, of which 1 were waited for; matrix products, arithmetic and copies ran while one was open for 0% of the time, Pallas kernels for 0%

profile of v1, /device:TPU:2, one launch (start us, length us, event | category | flops | bytes accessed | tf_op | source)
XLA Modules:
  0.0 240.5 jit_solution(10099737210066356943)
XLA Ops:
  7.2 0.0 reduce-scatter.2.cloned.1.call-start
  7.2 0.0 copy-start
  7.2 1.0 copy-done
  8.2 0.0 copy-start.1
  8.2 0.9 copy-done.1
  9.1 0.0 copy-start.2
  9.1 0.8 copy-done.2
  9.9 0.0 copy-start.3
  9.9 0.7 copy-done.3
  10.6 62.6 %shard_map.67 = (bf16[160,1024]{1,0:T(8,128)(2,1)S(1)}, bf16[160,768]{1,0:T(8,128)(2,1)S(1)}, bf16[1024,768]{1,0:T(8,128)(2,1)}) custom-call(bf16[160,1024]{1,0:T(8,128)(2,1)S(1)} %copy-done, bf16[160,768]{1,0:T(8,128)(2,1)S(1)} %copy-done.1, s32[1,160]{1,0:T(1,128)S(1)} %bitcast.1, bf16[32,768]{1,0:T(8,128)(2,1)S(1)} %copy-done.2), custom_call_target="tpu_custom_call" | custom-call | tf_op jit(solution)/shard_map/pallas_call | solution.py:262
  73.2 0.0 reduce-scatter.2.cloned.1.call-update
  73.3 94.9 %reduce-scatter.2.cloned.1.call-done = bf16[32,768]{1,0:T(8,128)(2,1)} async-done(((bf16[1024,768]{1,0:T(8,128)(2,1)}), bf16[32,768]{1,0:T(8,128)(2,1)}) %reduce-scatter.2.cloned.1.call-update) | async-done | bytes 49168 | tf_op jit(solution)/shard_map/reduce_scatter | solution.py:308
  168.1 63.4 %psum.7 = bf16[32,768]{1,0:T(8,128)(2,1)S(1)} all-reduce(bf16[32,768]{1,0:T(8,128)(2,1)} %reduce-scatter.2.cloned.1.call-done), channel_id=1, replica_groups=mesh['blk'=16,'group'=32] {'blk'}, use_global_device_ids=true, to_apply=%region_1.0 | all-reduce | flops 24576 | bytes 98304 | tf_op jit(solution)/shard_map/psum | solution.py:309
  231.6 0.7 convert_element_type.3
  232.2 0.7 copy.9
  232.9 0.7 copy.10
Async XLA Ops:
  7.2 161.0 %reduce-scatter.2.cloned.1.call-start = ((), (), s32[]{:S(2)}) async-start(), calls=%async_computation.1 | async-start | bytes 1622016 | tf_op jit(solution)/shard_map/reduce_scatter | solution.py:308
  7.2 1.0 copy-start
  8.2 0.9 copy-start.1
  9.1 0.8 copy-start.2
  9.9 0.7 copy-start.3
Sparse Core Ops, SparseCore 0:
  73.4 94.6 reduce-scatter.1

commit v2 on v1

--- a/solution.py
+++ b/solution.py
@@ -11,15 +11,17 @@
 SCALE = 16.0
 SHIFT = -4.0
 EPS = 1e-6
-ROWS, WIDE, COLS, HALF = 160, 1024, 768, 80
+ROWS, WIDE, COLS, HALF, MID = 160, 1024, 768, 80, 384
 
 
 def kernel(
-    audio_hbm, text_hbm, labels_ref, weight_hbm,
+    audio_hbm, text_hbm, labels_hbm, weight_hbm,
     audio_out, text_out, grad_out,
-    audio, text, texts, label_rows, pair_label, weight, units, unit_low, norms, d_audio, d_text,
-    dp_low, pair_dp, rs_out, rs_in, audio_res, text_res, grad_res,
+    labels, audio, audio_other, text, texts, label_rows, pair_label, weight, units, unit_low, norms, d_audio, d_text,
+    dp_low, dp_other, pair_dp, rs_out, rs_in, audio_res, text_res, grad_res,
+    gx, gx_in, gz, gz_in, gy, gy_in, gf, gf_in,
     load_sem, store_sem, gs, gr, ls, lr, w1s, w1r, w2s, w2r, wcs, wcr, ps, pr, rss, rsr,
+    cs, cr, xs, xr, zs, zr, ys, yr, fs, fr,
 ):
     blk, group = lax.axis_index("blk"), lax.axis_index("group")
     z_lo, y = blk // 8, blk % 8
@@ -34,8 +36,13 @@
     def at_z(step):
         return (blk, ((z_hi + step) % 4) * 8 + x * 2 + core)
 
+    def at_z_all(step):
+        there = (z_hi * 2 + z_lo + step) % 8
+        return ((there % 2) * 8 + y, (there // 2) * 8 + x * 2 + core)
+
     pair = ((1 - z_lo) * 8 + y, group)
     other = (blk, z_hi * 8 + x * 2 + (1 - core))
+    pair_other = ((1 - z_lo) * 8 + y, z_hi * 8 + x * 2 + (1 - core))
     ring = (at_y(1), at_y(-1))
     started = []
 
@@ -55,6 +62,7 @@
         pltpu.make_async_copy(text_hbm, text, load_sem.at[0]),
         pltpu.make_async_copy(weight_hbm, weight.at[z_hi, x * 2 + core], load_sem.at[1]),
         pltpu.make_async_copy(audio_hbm, audio.at[0], load_sem.at[2]),
+        pltpu.make_async_copy(labels_hbm, labels, load_sem.at[3]),
     ]
     for load in loads:
         load.start()
@@ -67,7 +75,8 @@
     loads[0].wait()
     raw = text[...].astype(F32)
     texts[0] = (raw / jnp.sqrt(jnp.sum(raw * raw, axis=-1, keepdims=True) + EPS)).astype(BF)
-    label_rows[0] = jnp.broadcast_to(labels_ref[...].astype(F32), (8, ROWS))
+    loads[3].wait()
+    label_rows[0] = jnp.broadcast_to(labels[...].reshape(1, ROWS).astype(F32), (8, ROWS))
     loads[1].wait()
     loads[2].wait()
     pl.semaphore_wait(barrier, len(friends))
@@ -105,6 +114,7 @@
         send(mine, mine, w1s.at[i - 1], w1r.at[i - 1], at_z(i))
     send(label_rows.at[0], pair_label, ps.at[0], pr.at[0], pair)
     send(audio.at[0], audio.at[1], ps.at[1], pr.at[1], pair)
+    send(audio.at[0], audio_other.at[0], cs.at[0], cr.at[0], other)
 
     def gather_hop(hop):
         for k in (0, 1):
@@ -141,6 +151,7 @@
         arrived(there, wcs.at[i], wcr.at[i])
     arrived(pair_label, ps.at[0], pr.at[0])
     arrived(audio.at[1], ps.at[1], pr.at[1])
+    send(audio.at[1], audio_other.at[1], cs.at[1], cr.at[1], other)
 
     whole = weight[...].reshape(WIDE, COLS)
     for i in (0, 1):
@@ -205,19 +216,27 @@
         total = d_audio[pl.ds(i * ROWS, ROWS), :]
         unit = units[i]
         share = (total - unit * jnp.sum(unit * total, axis=-1, keepdims=True)) / norms[i][:, 0:1]
-        dp_low[pl.ds(i * ROWS, ROWS), :] = share.astype(BF)
+        dp_low[0, i] = share[:, :MID].astype(BF)
+        dp_low[1, i] = share[:, MID:].astype(BF)
         if i == 0:
             d_audio[pl.ds(0, ROWS), :] = share
-    send(dp_low.at[pl.ds(ROWS, ROWS)], pair_dp, ps.at[2], pr.at[2], pair)
-
-    for i in range(4):
-        cut = pl.ds(i * 256, 256)
-        grad_res[cut, :] = (
-            lax.dot_general(audio[0, :, cut], dp_low[0:ROWS, :], (((0,), (0,)), ((), ())), preferred_element_type=F32)
-            + lax.dot_general(audio[1, :, cut], dp_low[ROWS:, :], (((0,), (0,)), ((), ())), preferred_element_type=F32)
-        ).astype(BF)
-    store_grad = pltpu.make_async_copy(grad_res, grad_out, store_sem.at[2])
-    store_grad.start()
+    send(dp_low.at[1 - core], dp_other, cs.at[2], cr.at[2], other)
+    send(dp_low.at[:, 1], pair_dp, ps.at[2], pr.at[2], pair)
+    for i in (0, 1):
+        arrived(audio_other.at[i], cs.at[i], cr.at[i])
+    arrived(dp_other, cs.at[2], cr.at[2])
+
+    for j in range(3):
+        cut = pl.ds(j * 128, 128)
+        total = jnp.zeros((WIDE, 128), F32)
+        for rows, cols in ((audio, dp_low.at[core]), (audio_other, dp_other)):
+            for i in (0, 1):
+                total += lax.dot_general(
+                    rows[i], cols[i, :, cut], (((0,), (0,)), ((), ())), preferred_element_type=F32
+                )
+        gx[j] = total.astype(BF).reshape(4, 4, 64, 128)
+        for i in (1, 3, 2):
+            send(gx.at[j, :, (x + i) % 4], gx_in.at[j, i - 1], xs.at[j, i - 1], xr.at[j, i - 1], at_x(i))
 
     for d in (0, 1):
         rs_send(d, 3, d)
@@ -225,7 +244,8 @@
         rs_send(d, 2, 1 - d)
 
     arrived(pair_dp, ps.at[2], pr.at[2])
-    dproj = (d_audio[0:ROWS, :] + pair_dp[...].astype(F32)).astype(BF)
+    both = jnp.concatenate([pair_dp[0], pair_dp[1]], axis=1).astype(F32)
+    dproj = (d_audio[0:ROWS, :] + both).astype(BF)
     audio_res[...] = lax.dot_general(
         dproj, weight[...].reshape(WIDE, COLS), (((1,), (1,)), ((), ())), preferred_element_type=F32
     ).astype(BF)
@@ -236,6 +256,15 @@
         rs_send(d, 2, d)
     for d in (0, 1):
         rs_send(d, 1, 1 - d)
+    for j in range(3):
+        total = gx[j, :, x].astype(F32)
+        for i in (1, 3, 2):
+            arrived(gx_in.at[j, i - 1], xs.at[j, i - 1], xr.at[j, i - 1])
+            total += gx_in[j, i - 1].astype(F32)
+        gz[:, :, j] = total.astype(BF).reshape(4, 2, 32, 128)
+    for i in (1, 7, 2, 6, 3, 5, 4):
+        there = (z_hi * 2 + z_lo + i) % 8
+        send(gz.at[there // 2, there % 2], gz_in.at[i - 1], zs.at[i - 1], zr.at[i - 1], at_z_all(i))
     for d in (0, 1):
         rs_send(d, 1, d)
     for k in (0, 1):
@@ -250,6 +279,52 @@
         ).astype(BF)
     store_text = pltpu.make_async_copy(text_res, text_out, store_sem.at[1])
     store_text.start()
+
+    total = gz[z_hi, z_lo].astype(F32)
+    for i in (1, 7, 2, 6, 3, 5, 4):
+        arrived(gz_in.at[i - 1], zs.at[i - 1], zr.at[i - 1])
+        total += gz_in[i - 1].astype(F32)
+    gy[...] = total.astype(BF)
+    for i in (1, 7, 2, 6, 3, 5, 4):
+        send(gy, gy_in.at[i - 1], ys.at[i - 1], yr.at[i - 1], at_y(i))
+    for i in (1, 7, 2, 6, 3, 5, 4):
+        arrived(gy_in.at[i - 1], ys.at[i - 1], yr.at[i - 1])
+        total += gy_in[i - 1].astype(F32)
+    gf[...] = total.astype(BF)
+
+    def final(to, k):
+        return pltpu.make_async_remote_copy(
+            src_ref=gf, dst_ref=gf_in.at[core], send_sem=fs.at[k], recv_sem=fr.at[core],
+            device_id=to, device_id_type=MESH,
+        )
+
+    def landed(half):
+        arrived(gf_in.at[half], fs.at[0], fr.at[half])
+
+    @pl.when(core == z_lo)
+    def _():
+        copy = final(pair, 0)
+        copy.start()
+        gf_in[core] = gf[...]
+        landed(1 - core)
+        copy.wait_send()
+
+    @pl.when(core != z_lo)
+    def _():
+        copy = final(pair_other, 0)
+        copy.start()
+        near = final(other, 1)
+        near.start()
+        landed(0)
+        landed(1)
+        copy.wait_send()
+        near.wait_send()
+
+    for half in (0, 1):
+        for j in range(3):
+            grad_res[:, pl.ds(half * MID + j * 128, 128)] = gf_in[half, j].astype(F32)
+    store_grad = pltpu.make_async_copy(grad_res, grad_out, store_sem.at[2])
+    store_grad.start()
     for copy in started:
         copy.wait_send()
     store_grad.wait()
@@ -259,21 +334,18 @@
 
 def on_device(audio, text, labels, audio_weight):
     dma = pltpu.SemaphoreType.DMA
-    audio_grad, text_grad, share = pl.pallas_call(
+    return pl.pallas_call(
         kernel,
         out_shape=(
             jax.ShapeDtypeStruct((ROWS, WIDE), BF),
             jax.ShapeDtypeStruct((ROWS, COLS), BF),
-            jax.ShapeDtypeStruct((WIDE, COLS), BF),
+            jax.ShapeDtypeStruct((32, COLS), F32),
         ),
-        in_specs=[
-            pl.BlockSpec(memory_space=pl.ANY),
-            pl.BlockSpec(memory_space=pl.ANY),
-            pl.BlockSpec(memory_space=pltpu.VMEM),
-            pl.BlockSpec(memory_space=pl.ANY),
-        ],
-        out_specs=[pl.BlockSpec(memory_space=pl.ANY)] * 3,
+        in_specs=[pl.BlockSpec(memory_space=pltpu.HBM)] * 4,
+        out_specs=[pl.BlockSpec(memory_space=pltpu.HBM)] * 3,
         scratch_shapes=[
+            pltpu.VMEM((ROWS,), jnp.int32),
+            pltpu.VMEM((2, ROWS, WIDE), BF),
             pltpu.VMEM((2, ROWS, WIDE), BF),
             pltpu.VMEM((ROWS, COLS), BF),
             pltpu.VMEM((8, ROWS, COLS), BF),
@@ -285,14 +357,23 @@
             pltpu.VMEM((2, ROWS, 128), F32),
             pltpu.VMEM((2 * ROWS, COLS), F32),
             pltpu.VMEM((8, ROWS, COLS), F32),
-            pltpu.VMEM((2 * ROWS, COLS), BF),
-            pltpu.VMEM((ROWS, COLS), BF),
+            pltpu.VMEM((2, 2, ROWS, MID), BF),
+            pltpu.VMEM((2, ROWS, MID), BF),
+            pltpu.VMEM((2, ROWS, MID), BF),
             pltpu.VMEM((2, 4, ROWS, COLS), BF),
             pltpu.VMEM((2, 4, ROWS, COLS), BF),
             pltpu.VMEM((ROWS, WIDE), BF),
             pltpu.VMEM((ROWS, COLS), BF),
-            pltpu.VMEM((WIDE, COLS), BF),
-            dma((3,)), dma((3,)),
+            pltpu.VMEM((32, COLS), F32),
+            pltpu.VMEM((3, 4, 4, 64, 128), BF),
+            pltpu.VMEM((3, 3, 4, 64, 128), BF),
+            pltpu.VMEM((4, 2, 3, 32, 128), BF),
+            pltpu.VMEM((7, 3, 32, 128), BF),
+            pltpu.VMEM((3, 32, 128), BF),
+            pltpu.VMEM((7, 3, 32, 128), BF),
+            pltpu.VMEM((3, 32, 128), BF),
+            pltpu.VMEM((2, 3, 32, 128), BF),
+            dma((4,)), dma((3,)),
             dma((2, 4, 2)), dma((2, 4, 2)),
             dma((2, 4)), dma((2, 4)),
             dma((3,)), dma((3,)),
@@ -300,14 +381,16 @@
             dma((4,)), dma((4,)),
             dma((3,)), dma((3,)),
             dma((2, 4, 2)), dma((2, 4, 2)),
+            dma((3,)), dma((3,)),
+            dma((3, 3)), dma((3, 3)),
+            dma((7,)), dma((7,)),
+            dma((7,)), dma((7,)),
+            dma((2,)), dma((2,)),
         ],
         compiler_params=pltpu.CompilerParams(
-            collective_id=0, has_side_effects=True, vmem_limit_bytes=48 * 2**20
+            collective_id=0, has_side_effects=True, vmem_limit_bytes=56 * 2**20
         ),
-    )(audio, text, labels.reshape(1, ROWS), audio_weight)
-    grad = lax.psum_scatter(share, "group", scatter_dimension=0, tiled=True)
-    weight_grad = lax.psum(grad, "blk").astype(F32)
-    return (audio_grad, text_grad, weight_grad)
+    )(audio, text, labels, audio_weight)
 
 
 def solution(mesh):

time: 241 us -> 78.7 us (0.33)
  the two profiles are of different devices: /device:TPU:2 before, /device:TPU:1 now
where the time goes in v2:
time: 78.7 us; the launch traced here: 78.5 us
  Pallas kernels  74.5 us (95%)
  local copies, waits for them, and re-layouts  3.37 us (4%)
    pallas_call x1, Pallas kernels, on_device(): pl.pallas_call(kernel, out_shape=(jax.ShapeDtypeStruct((ROWS, WIDE), BF),...  74.5 us
    unnamed x7, local copies, waits for them, and re-layouts  3.37 us

profile of v2, /device:TPU:1, one launch (start us, length us, event | category | flops | bytes accessed | tf_op | source)
XLA Modules:
  0.0 78.5 jit_solution(15701800021995844560)
XLA Ops:
  0.6 74.5 %shard_map.67 = (bf16[160,1024]{1,0:T(8,128)(2,1)}, bf16[160,768]{1,0:T(8,128)(2,1)}, f32[32,768]{1,0:T(8,128)}) custom-call(bf16[160,1024]{1,0:T(8,128)(2,1)} %audio_hbm.1, bf16[160,768]{1,0:T(8,128)(2,1)} %text_hbm.1, s32[160]{0:T(256)} %labels_hbm.1, bf16[32,768]{1,0:T(8,128)(2,1)} %weight_hbm.1), custom_call_target="tpu_custom_call" | custom-call | tf_op jit(solution)/shard_map/pallas_call | solution.py:337
  75.1 0.0 copy-start
  75.1 1.8 %copy.10 = bf16[160,1024]{1,0:T(8,128)(2,1)} copy(bf16[160,1024]{1,0:T(8,128)(2,1)} %get-tuple-element.6) | data formatting | bytes 655360
  76.9 0.0 copy-done
  76.9 0.0 copy-start.1
  76.9 0.7 copy.11
  77.6 0.3 copy-done.1
  77.8 0.6 copy.12
Async XLA Ops:
  75.1 1.8 %copy-start = (bf16[160,768]{1,0:T(8,128)(2,1)S(1)}, bf16[160,768]{1,0:T(8,128)(2,1)}, u32[]{:S(2)}) copy-start(bf16[160,768]{1,0:T(8,128)(2,1)} %get-tuple-element.7) | copy-start | bytes 737284
  76.9 1.0 %copy-start.1 = (f32[32,768]{1,0:T(8,128)S(1)}, f32[32,768]{1,0:T(8,128)}, u32[]{:S(2)}) copy-start(f32[32,768]{1,0:T(8,128)} %get-tuple-element.8) | copy-start | bytes 294916

commit v3 on v2

v3 whole, which is shorter than its diff:
```python
import jax
import jax.numpy as jnp
from jax import lax
from jax.experimental import pallas as pl
from jax.experimental.pallas import tpu as pltpu
from jax.sharding import PartitionSpec as P

MESH = pl.DeviceIdType.MESH
BF = jnp.bfloat16
F32 = jnp.float32
SCALE = 16.0
SHIFT = -4.0
EPS = 1e-6
ROWS, WIDE, COLS, HALF, MID = 160, 1024, 768, 80, 384
AROUND = (1, 7, 2, 6, 3, 5, 4)


def rows_by_columns(a, b):
    return lax.dot_general(a, b, (((1,), (1,)), ((), ())), preferred_element_type=F32)


def kernel(
    audio_hbm, text_hbm, labels_hbm, weight_hbm,
    audio_out, text_out, grad_out,
    labels, audio, audio_t, text, texts, label_rows, label_cols, pair_label, weight, units, unit_low, norms,
    d_audio, d_text, dp_low, dp_other, pair_dp, rs_out, rs_in, audio_res, text_res, grad_res,
    gx, gx_in, gz, gz_in, hz, hz_in, hx, hx_in, gy, gy_in, gf, gf_in,
    load_sem, store_sem, gs, gr, ls, lr, w1s, w1r, w2s, w2r, wcs, wcr, ps, pr, rss, rsr,
    cs, cr, xs, xr, zs, zr, hzs, hzr, hxs, hxr, ys, yr, fs, fr,
):
    blk, group = lax.axis_index("blk"), lax.axis_index("group")
    z_lo, y = blk // 8, blk % 8
    z_hi, x, core = group // 8, (group // 2) % 4, group % 2

    def at_y(step):
        return (z_lo * 8 + (y + step + 8) % 8, group)

    def at_x(step):
        return (blk, z_hi * 8 + ((x + step) % 4) * 2 + core)

    def at_z(step):
        there = (z_hi * 2 + z_lo + step + 8) % 8
        return ((there % 2) * 8 + y, (there // 2) * 8 + x * 2 + core)

    pair = ((1 - z_lo) * 8 + y, group)
    other = (blk, z_hi * 8 + x * 2 + (1 - core))
    pair_other = ((1 - z_lo) * 8 + y, z_hi * 8 + x * 2 + (1 - core))
    ring = (at_y(1), at_y(-1))
    started = []

    def send(src, dst, s, r, to):
        copy = pltpu.make_async_remote_copy(
            src_ref=src, dst_ref=dst, send_sem=s, recv_sem=r, device_id=to, device_id_type=MESH
        )
        copy.start()
        started.append(copy)

    def arrived(dst, s, r):
        pltpu.make_async_remote_copy(
            src_ref=dst, dst_ref=dst, send_sem=s, recv_sem=r, device_id=ring[0], device_id_type=MESH
        ).wait_recv()

    loads = [
        pltpu.make_async_copy(text_hbm, text, load_sem.at[0]),
        pltpu.make_async_copy(weight_hbm, weight.at[z_hi, x * 2 + core], load_sem.at[1]),
        pltpu.make_async_copy(labels_hbm, labels, load_sem.at[3]),
        pltpu.make_async_copy(audio_hbm, audio.at[0], load_sem.at[2]),
    ]
    for load in loads:
        load.start()

    barrier = pltpu.get_barrier_semaphore()
    away = 2 * z_lo - 1
    friends = ring + (pair, other, at_z(away), at_z(-2 * away), at_z(3 * away)) + tuple(at_x(i) for i in (1, 2, 3))
    for friend in friends:
        pl.semaphore_signal(barrier, inc=1, device_id=friend, device_id_type=MESH)

    loads[0].wait()
    raw = text[...].astype(F32)
    texts[0] = (raw / jnp.sqrt(jnp.sum(raw * raw, axis=-1, keepdims=True) + EPS)).astype(BF)
    loads[2].wait()
    label_rows[0] = jnp.broadcast_to(labels[...].reshape(1, ROWS).astype(F32), (8, ROWS))
    loads[1].wait()
    loads[3].wait()
    pl.semaphore_wait(barrier, len(friends))

    def part(k):
        return pl.ds(k * HALF, HALF)

    def slot_of(d, hop):
        return 2 * hop - 1 + d if hop < 4 else 7

    def gather_send(d, hop, k):
        src = 0 if hop == 1 else slot_of(d, hop - 1)
        send(
            texts.at[src, part(k)], texts.at[slot_of(d, hop), part(k)],
            gs.at[d, hop - 1, k], gr.at[d, hop - 1, k], ring[d],
        )

    def label_send(d, hop):
        src = 0 if hop == 1 else slot_of(d, hop - 1)
        send(
            label_rows.at[src], label_rows.at[slot_of(d, hop)],
            ls.at[d, hop - 1], lr.at[d, hop - 1], ring[d],
        )

    def gather_hop(hop, turn):
        for d in (0, 1):
            k = d if turn == 0 else 1 - d
            arrived(texts.at[slot_of(d, hop), part(k)], gs.at[d, hop - 1, k], gr.at[d, hop - 1, k])
            if hop < 3 or (hop == 3 and turn == 0):
                gather_send(d, hop + 1, k)

    diagonal = lax.broadcasted_iota(jnp.int32, (ROWS, ROWS), 0) == lax.broadcasted_iota(
        jnp.int32, (ROWS, ROWS), 1
    )

    def label_column(slot):
        row = label_rows[slot][0:1, :]
        column = jnp.sum(jnp.where(diagonal, row, 0.0), axis=1, keepdims=True)
        label_cols[slot] = jnp.broadcast_to(column, (ROWS, 128))

    def label_hop(hop):
        for d in (0, 1):
            if hop == 4 and d == 1:
                continue
            arrived(label_rows.at[slot_of(d, hop)], ls.at[d, hop - 1], lr.at[d, hop - 1])
            if hop < 3 or (hop == 3 and d == 0):
                label_send(d, hop + 1)
            label_column(slot_of(d, hop))

    def near_weight(e, i, side=core):
        return weight.at[(z_hi + 4 + away * (0, 1, -1, 2)[e]) % 4, ((x + 4 - i) % 4) * 2 + side]

    def weight_along_x(e):
        for i in (1, 3, 2):
            send(near_weight(e, 0), near_weight(e, 0), w2s.at[e, i - 1], w2r.at[e, i - 1], at_x(i))
        send(near_weight(e, 0), near_weight(e, 0), wcs.at[e, 0], wcr.at[e, 0], other)

    def weight_from_z(e):
        arrived(near_weight(e, 0), w1s.at[e - 1], w1r.at[e - 1])
        weight_along_x(e)

    def weight_from_x(e):
        for i in (1, 3, 2):
            there = near_weight(e, i)
            arrived(there, w2s.at[e, i - 1], w2r.at[e, i - 1])
            send(there, there, wcs.at[e, i], wcr.at[e, i], other)

    for d in (0, 1):
        gather_send(d, 1, d)
    mine = near_weight(0, 0)
    for e in (3, 2, 1):
        send(mine, mine, w1s.at[e - 1], w1r.at[e - 1], at_z(away * e))
    weight_along_x(0)
    for d in (0, 1):
        gather_send(d, 1, 1 - d)
        label_send(d, 1)
    send(label_rows.at[0], pair_label, ps.at[0], pr.at[0], pair)
    send(audio.at[0], audio.at[1], ps.at[1], pr.at[1], pair)
    send(audio.at[0], audio.at[2], cs.at[0], cr.at[0], other)
    label_column(0)
    audio_t[0] = audio[0].T

    gather_hop(1, 0)
    weight_from_z(1)
    weight_from_z(2)
    gather_hop(1, 1)
    weight_from_z(3)
    label_hop(1)
    weight_from_x(0)
    arrived(audio.at[2], cs.at[0], cr.at[0])
    audio_t[2] = audio[2].T
    gather_hop(2, 0)
    weight_from_x(1)
    weight_from_x(2)
    label_hop(2)
    gather_hop(2, 1)
    weight_from_x(3)
    arrived(pair_label, ps.at[0], pr.at[0])
    arrived(audio.at[1], ps.at[1], pr.at[1])
    send(audio.at[1], audio.at[3], cs.at[1], cr.at[1], other)
    audio_t[1] = audio[1].T
    gather_hop(3, 0)
    for e in range(4):
        for i in range(4):
            arrived(near_weight(e, i, 1 - core), wcs.at[e, i], wcr.at[e, i])

    whole = weight[...].reshape(WIDE, COLS)
    for i in (0, 1):
        proj = jnp.dot(audio[i], whole, preferred_element_type=F32)
        norm = jnp.sqrt(jnp.sum(proj * proj, axis=-1, keepdims=True) + EPS)
        unit = proj / norm
        units[i] = unit
        norms[i] = jnp.broadcast_to(norm, (ROWS, 128))
        unit_low[i] = unit.astype(BF)

    def blocks(first, count):
        many = count * ROWS
        rows = texts[first : first + count].reshape(many, COLS)
        row_labels = label_cols[first : first + count].reshape(many, 128)[:, 0:1]
        more = jnp.zeros((many, COLS), F32)
        for i in (0, 1):
            logits = SCALE * rows_by_columns(rows, unit_low[i]) + SHIFT
            own = label_rows[0][0:1, :] if i == 0 else pair_label[0:1, :]
            positive = (row_labels == own).astype(F32)
            pairs = (SCALE * (jax.nn.sigmoid(logits) - positive)).astype(BF)
            part_sum = lax.dot_general(pairs, rows, (((0,), (0,)), ((), ())), preferred_element_type=F32)
            d_audio[i] = part_sum if first == 0 else d_audio[i] + part_sum
            more += jnp.dot(pairs, unit_low[i], preferred_element_type=F32)
        d_text[first : first + count] = more.reshape(count, ROWS, COLS)

    def rs_send(r, turn):
        for d in (0, 1):
            k = d if turn == 0 else 1 - d
            slot = 7 if r == 4 else (2 * r if d == 0 else 2 * r - 1)
            value = d_text[slot, part(k), :]
            if r < 3 or (r == 3 and turn == 0):
                arrived(rs_in.at[d, r, part(k)], rss.at[d, r, k], rsr.at[d, r, k])
                value = value + rs_in[d, r, part(k), :].astype(F32)
            rs_out[d, r - 1, part(k), :] = value.astype(BF)
            send(
                rs_out.at[d, r - 1, part(k)], rs_in.at[d, r - 1, part(k)],
                rss.at[d, r - 1, k], rsr.at[d, r - 1, k], ring[d],
            )

    blocks(0, 3)
    label_hop(3)
    gather_hop(3, 1)
    blocks(3, 4)
    rs_send(3, 1)
    label_hop(4)
    arrived(audio.at[3], cs.at[1], cr.at[1])
    audio_t[3] = audio[3].T
    gather_hop(4, 0)
    blocks(7, 1)

    for i in (1, 0):
        total = d_audio[i]
        unit = units[i]
        share = (total - unit * jnp.sum(unit * total, axis=-1, keepdims=True)) / norms[i][:, 0:1]
        dp_low[0, i] = share[:, :MID].astype(BF)
        dp_low[1, i] = share[:, MID:].astype(BF)
        if i == 0:
            d_audio[0] = share
    send(dp_low.at[1 - core], dp_other, cs.at[2], cr.at[2], other)
    rs_send(4, 0)
    arrived(dp_other, cs.at[2], cr.at[2])

    def product(cut):
        total = jnp.dot(audio_t[0], dp_low[core, 0, :, cut], preferred_element_type=F32)
        total += jnp.dot(audio_t[1], dp_low[core, 1, :, cut], preferred_element_type=F32)
        total += jnp.dot(audio_t[2], dp_other[0, :, cut], preferred_element_type=F32)
        return total + jnp.dot(audio_t[3], dp_other[1, :, cut], preferred_element_type=F32)

    hz[...] = product(pl.ds(256, 128)).astype(BF).reshape(4, 4, 2, 32, 128)
    for i in AROUND:
        there = (z_hi * 2 + z_lo + i) % 8
        send(hz.at[there // 2, :, there % 2], hz_in.at[i - 1], hzs.at[i - 1], hzr.at[i - 1], at_z(i))
    for j in (0, 1):
        gx[j] = product(pl.ds(j * 128, 128)).astype(BF).reshape(4, 4, 64, 128)
        for i in (2, 1, 3):
            send(gx.at[j, :, (x + i) % 4], gx_in.at[j, i - 1], xs.at[j, i - 1], xr.at[j, i - 1], at_x(i))

    def along_z(j):
        total = gx[j, :, x].astype(F32)
        for i in (1, 3, 2):
            arrived(gx_in.at[j, i - 1], xs.at[j, i - 1], xr.at[j, i - 1])
            total += gx_in[j, i - 1].astype(F32)
        gz[j] = total.astype(BF).reshape(4, 2, 32, 128)
        for i in AROUND:
            there = (z_hi * 2 + z_lo + i) % 8
            send(gz.at[j, there // 2, there % 2], gz_in.at[j, i - 1], zs.at[j, i - 1], zr.at[j, i - 1], at_z(i))

    def along_x():
        total = hz[z_hi, :, z_lo].astype(F32)
        for i in AROUND:
            arrived(hz_in.at[i - 1], hzs.at[i - 1], hzr.at[i - 1])
            total += hz_in[i - 1].astype(F32)
        hx[...] = total.astype(BF)
        for i in (2, 1, 3):
            send(hx.at[(x + i) % 4], hx_in.at[i - 1], hxs.at[i - 1], hxr.at[i - 1], at_x(i))

    def along_y(j):
        if j < 2:
            total = gz[j, z_hi, z_lo].astype(F32)
            for i in AROUND:
                arrived(gz_in.at[j, i - 1], zs.at[j, i - 1], zr.at[j, i - 1])
                total += gz_in[j, i - 1].astype(F32)
        else:
            total = hx[x].astype(F32)
            for i in (1, 3, 2):
                arrived(hx_in.at[i - 1], hxs.at[i - 1], hxr.at[i - 1])
                total += hx_in[i - 1].astype(F32)
        gy[j] = total.astype(BF)
        for i in AROUND:
            send(gy.at[j], gy_in.at[j, i - 1], ys.at[j, i - 1], yr.at[j, i - 1], at_y(i))

    def complete(j):
        total = gy[j].astype(F32)
        for i in AROUND:
            arrived(gy_in.at[j, i - 1], ys.at[j, i - 1], yr.at[j, i - 1])
            total += gy_in[j, i - 1].astype(F32)
        gf[j] = total.astype(BF)

    rs_send(2, 1)
    rs_send(3, 0)
    along_z(0)
    rs_send(1, 1)
    rs_send(2, 0)
    along_z(1)
    send(dp_low.at[:, 1], pair_dp, ps.at[2], pr.at[2], pair)
    along_x()

    along_y(0)
    along_y(2)
    rs_send(1, 0)
    along_y(1)

    for turn in (1, 0):
        for k in (0, 1):
            d = k if turn == 0 else 1 - k
            arrived(rs_in.at[d, 0, part(k)], rss.at[d, 0, k], rsr.at[d, 0, k])
    raw = text[...].astype(F32)
    norm = jnp.sqrt(jnp.sum(raw * raw, axis=-1, keepdims=True) + EPS)
    unit = raw / norm
    total = d_text[0] + rs_in[0, 0].astype(F32) + rs_in[1, 0].astype(F32)
    text_res[...] = ((total - unit * jnp.sum(unit * total, axis=-1, keepdims=True)) / norm).astype(BF)
    store_text = pltpu.make_async_copy(text_res, text_out, store_sem.at[1])
    store_text.start()

    arrived(pair_dp, ps.at[2], pr.at[2])
    both = jnp.concatenate([pair_dp[0], pair_dp[1]], axis=1).astype(F32)
    dproj = (d_audio[0] + both).astype(BF)
    audio_res[...] = rows_by_columns(dproj, weight[...].reshape(WIDE, COLS)).astype(BF)
    store_audio = pltpu.make_async_copy(audio_res, audio_out, store_sem.at[0])
    store_audio.start()

    complete(0)
    complete(2)
    complete(1)

    def final(to, k):
        return pltpu.make_async_remote_copy(
            src_ref=gf, dst_ref=gf_in.at[core], send_sem=fs.at[k], recv_sem=fr.at[core],
            device_id=to, device_id_type=MESH,
        )

    def landed(half):
        arrived(gf_in.at[half], fs.at[0], fr.at[half])

    @pl.when(core == z_lo)
    def _():
        copy = final(pair, 0)
        copy.start()
        gf_in[core] = gf[...]
        landed(1 - core)
        copy.wait_send()

    @pl.when(core != z_lo)
    def _():
        copy = final(pair_other, 0)
        copy.start()
        near = final(other, 1)
        near.start()
        landed(0)
        landed(1)
        copy.wait_send()
        near.wait_send()

    for half in (0, 1):
        for j in range(3):
            grad_res[:, pl.ds(half * MID + j * 128, 128)] = gf_in[half, j].astype(F32)
    store_grad = pltpu.make_async_copy(grad_res, grad_out, store_sem.at[2])
    store_grad.start()
    for copy in started:
        copy.wait_send()
    store_audio.wait()
    store_text.wait()
    store_grad.wait()


def on_device(audio, text, labels, audio_weight):
    dma = pltpu.SemaphoreType.DMA
    twice = lambda *shape: [dma(shape), dma(shape)]
    return pl.pallas_call(
        kernel,
        out_shape=(
            jax.ShapeDtypeStruct((ROWS, WIDE), BF),
            jax.ShapeDtypeStruct((ROWS, COLS), BF),
            jax.ShapeDtypeStruct((32, COLS), F32),
        ),
        in_specs=[pl.BlockSpec(memory_space=pltpu.HBM)] * 4,
        out_specs=[pl.BlockSpec(memory_space=pltpu.HBM)] * 3,
        scratch_shapes=[
            pltpu.VMEM((ROWS,), jnp.int32),
            pltpu.VMEM((4, ROWS, WIDE), BF),
            pltpu.VMEM((4, WIDE, ROWS), BF),
            pltpu.VMEM((ROWS, COLS), BF),
            pltpu.VMEM((8, ROWS, COLS), BF),
            pltpu.VMEM((8, 8, ROWS), F32),
            pltpu.VMEM((8, ROWS, 128), F32),
            pltpu.VMEM((8, ROWS), F32),
            pltpu.VMEM((4, 8, 32, COLS), BF),
            pltpu.VMEM((2, ROWS, COLS), F32),
            pltpu.VMEM((2, ROWS, COLS), BF),
            pltpu.VMEM((2, ROWS, 128), F32),
            pltpu.VMEM((2, ROWS, COLS), F32),
            pltpu.VMEM((8, ROWS, COLS), F32),
            pltpu.VMEM((2, 2, ROWS, MID), BF),
            pltpu.VMEM((2, ROWS, MID), BF),
            pltpu.VMEM((2, ROWS, MID), BF),
            pltpu.VMEM((2, 4, ROWS, COLS), BF),
            pltpu.VMEM((2, 4, ROWS, COLS), BF),
            pltpu.VMEM((ROWS, WIDE), BF),
            pltpu.VMEM((ROWS, COLS), BF),
            pltpu.VMEM((32, COLS), F32),
            pltpu.VMEM((2, 4, 4, 64, 128), BF),
            pltpu.VMEM((2, 3, 4, 64, 128), BF),
            pltpu.VMEM((2, 4, 2, 32, 128), BF),
            pltpu.VMEM((2, 7, 32, 128), BF),
            pltpu.VMEM((4, 4, 2, 32, 128), BF),
            pltpu.VMEM((7, 4, 32, 128), BF),
            pltpu.VMEM((4, 32, 128), BF),
            pltpu.VMEM((3, 32, 128), BF),
            pltpu.VMEM((3, 32, 128), BF),
            pltpu.VMEM((3, 7, 32, 128), BF),
            pltpu.VMEM((3, 32, 128), BF),
            pltpu.VMEM((2, 3, 32, 128), BF),
            dma((4,)), dma((3,)),
            *twice(2, 4, 2), *twice(2, 4),
            *twice(3), *twice(4, 3), *twice(4, 4),
            *twice(3), *twice(2, 4, 2),
            *twice(3), *twice(2, 3), *twice(2, 7), *twice(7), *twice(3), *twice(3, 7), *twice(2),
        ],
        compiler_params=pltpu.CompilerParams(
            collective_id=0, has_side_effects=True, vmem_limit_bytes=56 * 2**20
        ),
    )(audio, text, labels, audio_weight)


def solution(mesh):
    rows = P(("blk", "group"), None)
    return jax.shard_map(
        on_device,
        mesh=mesh,
        in_specs=(rows, rows, P(("blk", "group")), P("group", None)),
        out_specs=(rows, rows, P("group", None)),
        check_vma=False,
    )
```

time: 78.7 us -> 72.3 us (0.919)
  Pallas kernels: 74.5 us -> 68.1 us
    pallas_call x1, Pallas kernels: 74.5 us -> 68.1 us  [on_device(): pl.pallas_call(kernel, out_shape=(jax.ShapeDtypeStruct((ROWS, WIDE), BF),...]
where the time goes in v3:
time: 72.3 us; the launch traced here: 72.1 us
  Pallas kernels  68.1 us (94%)
  local copies, waits for them, and re-layouts  3.37 us (5%)
    pallas_call x1, Pallas kernels, on_device(): pl.pallas_call(kernel, out_shape=(jax.ShapeDtypeStruct((ROWS, WIDE), BF),...  68.1 us
    unnamed x7, local copies, waits for them, and re-layouts  3.37 us

profile of v3, /device:TPU:1, one launch (start us, length us, event | category | flops | bytes accessed | tf_op | source)
XLA Modules:
  0.0 72.1 jit_solution(12290826005055188108)
XLA Ops:
  0.6 68.1 %shard_map.67 = (bf16[160,1024]{1,0:T(8,128)(2,1)}, bf16[160,768]{1,0:T(8,128)(2,1)}, f32[32,768]{1,0:T(8,128)}) custom-call(bf16[160,1024]{1,0:T(8,128)(2,1)} %audio_hbm.1, bf16[160,768]{1,0:T(8,128)(2,1)} %text_hbm.1, s32[160]{0:T(256)} %labels_hbm.1, bf16[32,768]{1,0:T(8,128)(2,1)} %weight_hbm.1), custom_call_target="tpu_custom_call" | custom-call | tf_op jit(solution)/shard_map/pallas_call | solution.py:386
  68.7 0.0 copy-start
  68.7 1.8 %copy.10 = bf16[160,1024]{1,0:T(8,128)(2,1)} copy(bf16[160,1024]{1,0:T(8,128)(2,1)} %get-tuple-element.6) | data formatting | bytes 655360
  70.5 0.0 copy-done
  70.5 0.0 copy-start.1
  70.5 0.7 copy.11
  71.2 0.3 copy-done.1
  71.5 0.6 copy.12
Async XLA Ops:
  68.7 1.8 %copy-start = (bf16[160,768]{1,0:T(8,128)(2,1)S(1)}, bf16[160,768]{1,0:T(8,128)(2,1)}, u32[]{:S(2)}) copy-start(bf16[160,768]{1,0:T(8,128)(2,1)} %get-tuple-element.7) | copy-start | bytes 737284
  70.5 1.0 %copy-start.1 = (f32[32,768]{1,0:T(8,128)S(1)}, f32[32,768]{1,0:T(8,128)}, u32[]{:S(2)}) copy-start(f32[32,768]{1,0:T(8,128)} %get-tuple-element.8) | copy-start | bytes 294916

commit v4 on v3

--- a/solution.py
+++ b/solution.py
@@ -199,16 +199,19 @@
         many = count * ROWS
         rows = texts[first : first + count].reshape(many, COLS)
         row_labels = label_cols[first : first + count].reshape(many, 128)[:, 0:1]
-        more = jnp.zeros((many, COLS), F32)
+        pairs = []
         for i in (0, 1):
             logits = SCALE * rows_by_columns(rows, unit_low[i]) + SHIFT
             own = label_rows[0][0:1, :] if i == 0 else pair_label[0:1, :]
             positive = (row_labels == own).astype(F32)
-            pairs = (SCALE * (jax.nn.sigmoid(logits) - positive)).astype(BF)
-            part_sum = lax.dot_general(pairs, rows, (((0,), (0,)), ((), ())), preferred_element_type=F32)
-            d_audio[i] = part_sum if first == 0 else d_audio[i] + part_sum
-            more += jnp.dot(pairs, unit_low[i], preferred_element_type=F32)
-        d_text[first : first + count] = more.reshape(count, ROWS, COLS)
+            pairs.append((SCALE * (jax.nn.sigmoid(logits) - positive)).astype(BF))
+        d_text[first : first + count] = (
+            jnp.dot(pairs[0], unit_low[0], preferred_element_type=F32)
+            + jnp.dot(pairs[1], unit_low[1], preferred_element_type=F32)
+        ).reshape(count, ROWS, COLS)
+        for i in (0, 1):
+            more = lax.dot_general(pairs[i], rows, (((0,), (0,)), ((), ())), preferred_element_type=F32)
+            d_audio[i] = more if first == 0 else d_audio[i] + more
 
     def rs_send(r, turn):
         for d in (0, 1):
@@ -234,6 +237,7 @@
     audio_t[3] = audio[3].T
     gather_hop(4, 0)
     blocks(7, 1)
+    rs_send(4, 0)
 
     for i in (1, 0):
         total = d_audio[i]
@@ -244,7 +248,6 @@
         if i == 0:
             d_audio[0] = share
     send(dp_low.at[1 - core], dp_other, cs.at[2], cr.at[2], other)
-    rs_send(4, 0)
     arrived(dp_other, cs.at[2], cr.at[2])
 
     def product(cut):
@@ -253,14 +256,15 @@
         total += jnp.dot(audio_t[2], dp_other[0, :, cut], preferred_element_type=F32)
         return total + jnp.dot(audio_t[3], dp_other[1, :, cut], preferred_element_type=F32)
 
+    first = product(pl.ds(0, 256)).astype(BF)
+    for j in (0, 1):
+        gx[j] = first[:, j * 128 : j * 128 + 128].reshape(4, 4, 64, 128)
+        for i in (2, 1, 3):
+            send(gx.at[j, :, (x + i) % 4], gx_in.at[j, i - 1], xs.at[j, i - 1], xr.at[j, i - 1], at_x(i))
     hz[...] = product(pl.ds(256, 128)).astype(BF).reshape(4, 4, 2, 32, 128)
     for i in AROUND:
         there = (z_hi * 2 + z_lo + i) % 8
         send(hz.at[there // 2, :, there % 2], hz_in.at[i - 1], hzs.at[i - 1], hzr.at[i - 1], at_z(i))
-    for j in (0, 1):
-        gx[j] = product(pl.ds(j * 128, 128)).astype(BF).reshape(4, 4, 64, 128)
-        for i in (2, 1, 3):
-            send(gx.at[j, :, (x + i) % 4], gx_in.at[j, i - 1], xs.at[j, i - 1], xr.at[j, i - 1], at_x(i))
 
     def along_z(j):
         total = gx[j, :, x].astype(F32)
@@ -306,16 +310,45 @@
     rs_send(2, 1)
     rs_send(3, 0)
     along_z(0)
+    along_z(1)
+    send(dp_low.at[:, 1], pair_dp, ps.at[2], pr.at[2], pair)
     rs_send(1, 1)
     rs_send(2, 0)
-    along_z(1)
-    send(dp_low.at[:, 1], pair_dp, ps.at[2], pr.at[2], pair)
     along_x()
-
     along_y(0)
     along_y(2)
+    along_y(1)
     rs_send(1, 0)
-    along_y(1)
+
+    complete(0)
+    complete(2)
+    complete(1)
+
+    def final(to, k):
+        return pltpu.make_async_remote_copy(
+            src_ref=gf, dst_ref=gf_in.at[core], send_sem=fs.at[k], recv_sem=fr.at[core],
+            device_id=to, device_id_type=MESH,
+        )
+
+    def landed(half):
+        arrived(gf_in.at[half], fs.at[0], fr.at[half])
+
+    @pl.when(core == z_lo)
+    def _():
+        final(pair, 0).start()
+        gf_in[core] = gf[...]
+
+    @pl.when(core != z_lo)
+    def _():
+        final(pair_other, 0).start()
+        final(other, 1).start()
+
+    arrived(pair_dp, ps.at[2], pr.at[2])
+    both = jnp.concatenate([pair_dp[0], pair_dp[1]], axis=1).astype(F32)
+    dproj = (d_audio[0] + both).astype(BF)
+    audio_res[...] = rows_by_columns(dproj, weight[...].reshape(WIDE, COLS)).astype(BF)
+    store_audio = pltpu.make_async_copy(audio_res, audio_out, store_sem.at[0])
+    store_audio.start()
 
     for turn in (1, 0):
         for k in (0, 1):
@@ -329,44 +362,17 @@
     store_text = pltpu.make_async_copy(text_res, text_out, store_sem.at[1])
     store_text.start()
 
-    arrived(pair_dp, ps.at[2], pr.at[2])
-    both = jnp.concatenate([pair_dp[0], pair_dp[1]], axis=1).astype(F32)
-    dproj = (d_audio[0] + both).astype(BF)
-    audio_res[...] = rows_by_columns(dproj, weight[...].reshape(WIDE, COLS)).astype(BF)
-    store_audio = pltpu.make_async_copy(audio_res, audio_out, store_sem.at[0])
-    store_audio.start()
-
-    complete(0)
-    complete(2)
-    complete(1)
-
-    def final(to, k):
-        return pltpu.make_async_remote_copy(
-            src_ref=gf, dst_ref=gf_in.at[core], send_sem=fs.at[k], recv_sem=fr.at[core],
-            device_id=to, device_id_type=MESH,
-        )
-
-    def landed(half):
-        arrived(gf_in.at[half], fs.at[0], fr.at[half])
-
     @pl.when(core == z_lo)
     def _():
-        copy = final(pair, 0)
-        copy.start()
-        gf_in[core] = gf[...]
         landed(1 - core)
-        copy.wait_send()
+        final(pair, 0).wait_send()
 
     @pl.when(core != z_lo)
     def _():
-        copy = final(pair_other, 0)
-        copy.start()
-        near = final(other, 1)
-        near.start()
         landed(0)
         landed(1)
-        copy.wait_send()
-        near.wait_send()
+        final(pair_other, 0).wait_send()
+        final(other, 1).wait_send()
 
     for half in (0, 1):
         for j in range(3):
@@ -380,16 +386,30 @@
     store_grad.wait()
 
 
+def hand_over(audio_in, text_in, grad_in, audio_out, text_out, grad_out, audio, text, grad, sems):
+    ways = ((audio_in, audio, audio_out), (text_in, text, text_out), (grad_in, grad, grad_out))
+    loads = [pltpu.make_async_copy(src, by, sems.at[i]) for i, (src, by, _) in enumerate(ways)]
+    stores = [pltpu.make_async_copy(by, dst, sems.at[3 + i]) for i, (_, by, dst) in enumerate(ways)]
+    for load in loads:
+        load.start()
+    for load, store in zip(loads, stores):
+        load.wait()
+        store.start()
+    for store in stores:
+        store.wait()
+
+
 def on_device(audio, text, labels, audio_weight):
     dma = pltpu.SemaphoreType.DMA
     twice = lambda *shape: [dma(shape), dma(shape)]
-    return pl.pallas_call(
+    shapes = (
+        jax.ShapeDtypeStruct((ROWS, WIDE), BF),
+        jax.ShapeDtypeStruct((ROWS, COLS), BF),
+        jax.ShapeDtypeStruct((32, COLS), F32),
+    )
+    results = pl.pallas_call(
         kernel,
-        out_shape=(
-            jax.ShapeDtypeStruct((ROWS, WIDE), BF),
-            jax.ShapeDtypeStruct((ROWS, COLS), BF),
-            jax.ShapeDtypeStruct((32, COLS), F32),
-        ),
+        out_shape=shapes,
         in_specs=[pl.BlockSpec(memory_space=pltpu.HBM)] * 4,
         out_specs=[pl.BlockSpec(memory_space=pltpu.HBM)] * 3,
         scratch_shapes=[
@@ -437,6 +457,19 @@
             collective_id=0, has_side_effects=True, vmem_limit_bytes=56 * 2**20
         ),
     )(audio, text, labels, audio_weight)
+    return pl.pallas_call(
+        hand_over,
+        out_shape=shapes,
+        in_specs=[pl.BlockSpec(memory_space=pl.ANY)] * 3,
+        out_specs=[pl.BlockSpec(memory_space=pl.ANY)] * 3,
+        scratch_shapes=[
+            pltpu.VMEM((ROWS, WIDE), BF),
+            pltpu.VMEM((ROWS, COLS), BF),
+            pltpu.VMEM((32, COLS), F32),
+            dma((6,)),
+        ],
+        compiler_params=pltpu.CompilerParams(vmem_limit_bytes=56 * 2**20),
+    )(*results)
 
 
 def solution(mesh):

time: 72.3 us -> 69 us (0.954)
  local copies, waits for them, and re-layouts: 3.37 us -> 0 us
    unnamed x7 -> x0, local copies, waits for them, and re-layouts: 3.37 us -> none
    pallas_call x1 -> x2, Pallas kernels: 68.1 us -> 68.2 us  [the longest x1 66.3 us: on_device(): pl.pallas_call(kernel, out_shape=shapes, in_specs=[pl.BlockSpec(memory_sp...]
where the time goes in v4:
time: 69 us; the launch traced here: 68.8 us
  Pallas kernels  68.2 us (99%)
    pallas_call x1, Pallas kernels, on_device(): pl.pallas_call(kernel, out_shape=shapes, in_specs=[pl.BlockSpec(memory_sp...  66.3 us
    pallas_call x1, Pallas kernels, on_device(): pl.pallas_call(hand_over, out_shape=shapes, in_specs=[pl.BlockSpec(memory...  1.85 us

profile of v4, /device:TPU:1, one launch (start us, length us, event | category | flops | bytes accessed | tf_op | source)
XLA Modules:
  0.0 68.8 jit_solution(7278109933723757754)
XLA Ops:
  0.6 66.3 %shard_map.67 = (bf16[160,1024]{1,0:T(8,128)(2,1)}, bf16[160,768]{1,0:T(8,128)(2,1)}, f32[32,768]{1,0:T(8,128)}) custom-call(bf16[160,1024]{1,0:T(8,128)(2,1)} %audio_hbm.1, bf16[160,768]{1,0:T(8,128)(2,1)} %text_hbm.1, s32[160]{0:T(256)} %labels_hbm.1, bf16[32,768]{1,0:T(8,128)(2,1)} %weight_hbm.1), custom_call_target="tpu_custom_call" | custom-call | tf_op jit(solution)/shard_map/pallas_call | solution.py:410
  67.0 1.9 %shard_map.68 = (bf16[160,1024]{1,0:T(8,128)(2,1)}, bf16[160,768]{1,0:T(8,128)(2,1)}, f32[32,768]{1,0:T(8,128)}) custom-call(bf16[160,1024]{1,0:T(8,128)(2,1)} %get-tuple-element.6.audio_in, bf16[160,768]{1,0:T(8,128)(2,1)} %get-tuple-element.7.text_in, f32[32,768]{1,0:T(8,128)} %get-tuple-element.8.grad_in), custom_call_target="tpu_custom_call" | custom-call | tf_op jit(solution)/shard_map/pallas_call | solution.py:460

commit v5 on v4

--- a/solution.py
+++ b/solution.py
@@ -24,7 +24,7 @@
     audio_out, text_out, grad_out,
     labels, audio, audio_t, text, texts, label_rows, label_cols, pair_label, weight, units, unit_low, norms,
     d_audio, d_text, dp_low, dp_other, pair_dp, rs_out, rs_in, audio_res, text_res, grad_res,
-    gx, gx_in, gz, gz_in, hz, hz_in, hx, hx_in, gy, gy_in, gf, gf_in,
+    early, gx, gx_in, gz, gz_in, hz, hz_in, hx, hx_in, gy, gy_in, gf, gf_in,
     load_sem, store_sem, gs, gr, ls, lr, w1s, w1r, w2s, w2r, wcs, wcr, ps, pr, rss, rsr,
     cs, cr, xs, xr, zs, zr, hzs, hzr, hxs, hxr, ys, yr, fs, fr,
 ):
@@ -59,6 +59,12 @@
         pltpu.make_async_remote_copy(
             src_ref=dst, dst_ref=dst, send_sem=s, recv_sem=r, device_id=ring[0], device_id_type=MESH
         ).wait_recv()
+
+    barrier = pltpu.get_barrier_semaphore()
+    away = 2 * z_lo - 1
+    friends = ring + (pair, other, at_z(away), at_z(-2 * away), at_z(3 * away)) + tuple(at_x(i) for i in (1, 2, 3))
+    for friend in friends:
+        pl.semaphore_signal(barrier, inc=1, device_id=friend, device_id_type=MESH)
 
     loads = [
         pltpu.make_async_copy(text_hbm, text, load_sem.at[0]),
@@ -68,12 +74,6 @@
     ]
     for load in loads:
         load.start()
-
-    barrier = pltpu.get_barrier_semaphore()
-    away = 2 * z_lo - 1
-    friends = ring + (pair, other, at_z(away), at_z(-2 * away), at_z(3 * away)) + tuple(at_x(i) for i in (1, 2, 3))
-    for friend in friends:
-        pl.semaphore_signal(barrier, inc=1, device_id=friend, device_id_type=MESH)
 
     loads[0].wait()
     raw = text[...].astype(F32)
@@ -176,19 +176,29 @@
     weight_from_x(2)
     label_hop(2)
     gather_hop(2, 1)
-    weight_from_x(3)
     arrived(pair_label, ps.at[0], pr.at[0])
     arrived(audio.at[1], ps.at[1], pr.at[1])
     send(audio.at[1], audio.at[3], cs.at[1], cr.at[1], other)
     audio_t[1] = audio[1].T
-    gather_hop(3, 0)
-    for e in range(4):
+    def weight_rows(e):
         for i in range(4):
             arrived(near_weight(e, i, 1 - core), wcs.at[e, i], wcr.at[e, i])
-
-    whole = weight[...].reshape(WIDE, COLS)
+        there = (z_hi + 4 + away * (0, 1, -1, 2)[e]) % 4
+        for i in (0, 1):
+            more = jnp.dot(
+                audio[i, :, pl.ds(pl.multiple_of(there * 256, 256), 256)],
+                weight[there].reshape(256, COLS),
+                preferred_element_type=F32,
+            )
+            units[i] = more if e == 0 else units[i] + more
+
+    for e in range(3):
+        weight_rows(e)
+    weight_from_x(3)
+    gather_hop(3, 0)
+    weight_rows(3)
     for i in (0, 1):
-        proj = jnp.dot(audio[i], whole, preferred_element_type=F32)
+        proj = units[i]
         norm = jnp.sqrt(jnp.sum(proj * proj, axis=-1, keepdims=True) + EPS)
         unit = proj / norm
         units[i] = unit
@@ -211,7 +221,7 @@
         ).reshape(count, ROWS, COLS)
         for i in (0, 1):
             more = lax.dot_general(pairs[i], rows, (((0,), (0,)), ((), ())), preferred_element_type=F32)
-            d_audio[i] = more if first == 0 else d_audio[i] + more
+            d_audio[i] = more if first == 3 else d_audio[i] + more
 
     def rs_send(r, turn):
         for d in (0, 1):
@@ -227,11 +237,11 @@
                 rss.at[d, r - 1, k], rsr.at[d, r - 1, k], ring[d],
             )
 
-    blocks(0, 3)
     label_hop(3)
     gather_hop(3, 1)
     blocks(3, 4)
     rs_send(3, 1)
+    blocks(0, 3)
     label_hop(4)
     arrived(audio.at[3], cs.at[1], cr.at[1])
     audio_t[3] = audio[3].T
@@ -247,21 +257,26 @@
         dp_low[1, i] = share[:, MID:].astype(BF)
         if i == 0:
             d_audio[0] = share
-    send(dp_low.at[1 - core], dp_other, cs.at[2], cr.at[2], other)
-    arrived(dp_other, cs.at[2], cr.at[2])
-
-    def product(cut):
+        send(dp_low.at[1 - core, i], dp_other.at[i], cs.at[2 + i], cr.at[2 + i], other)
+
+    def of_core(cut):
         total = jnp.dot(audio_t[0], dp_low[core, 0, :, cut], preferred_element_type=F32)
-        total += jnp.dot(audio_t[1], dp_low[core, 1, :, cut], preferred_element_type=F32)
+        return total + jnp.dot(audio_t[1], dp_low[core, 1, :, cut], preferred_element_type=F32)
+
+    early[...] = of_core(pl.ds(0, 256))
+    for i in (1, 0):
+        arrived(dp_other.at[i], cs.at[2 + i], cr.at[2 + i])
+
+    def product(cut, total):
         total += jnp.dot(audio_t[2], dp_other[0, :, cut], preferred_element_type=F32)
         return total + jnp.dot(audio_t[3], dp_other[1, :, cut], preferred_element_type=F32)
 
-    first = product(pl.ds(0, 256)).astype(BF)
+    first = product(pl.ds(0, 256), early[...]).astype(BF)
     for j in (0, 1):
         gx[j] = first[:, j * 128 : j * 128 + 128].reshape(4, 4, 64, 128)
         for i in (2, 1, 3):
             send(gx.at[j, :, (x + i) % 4], gx_in.at[j, i - 1], xs.at[j, i - 1], xr.at[j, i - 1], at_x(i))
-    hz[...] = product(pl.ds(256, 128)).astype(BF).reshape(4, 4, 2, 32, 128)
+    hz[...] = product(pl.ds(256, 128), of_core(pl.ds(256, 128))).astype(BF).reshape(4, 4, 2, 32, 128)
     for i in AROUND:
         there = (z_hi * 2 + z_lo + i) % 8
         send(hz.at[there // 2, :, there % 2], hz_in.at[i - 1], hzs.at[i - 1], hzr.at[i - 1], at_z(i))
@@ -435,6 +450,7 @@
             pltpu.VMEM((ROWS, WIDE), BF),
             pltpu.VMEM((ROWS, COLS), BF),
             pltpu.VMEM((32, COLS), F32),
+            pltpu.VMEM((WIDE, 256), F32),
             pltpu.VMEM((2, 4, 4, 64, 128), BF),
             pltpu.VMEM((2, 3, 4, 64, 128), BF),
             pltpu.VMEM((2, 4, 2, 32, 128), BF),
@@ -451,7 +467,7 @@
             *twice(2, 4, 2), *twice(2, 4),
             *twice(3), *twice(4, 3), *twice(4, 4),
             *twice(3), *twice(2, 4, 2),
-            *twice(3), *twice(2, 3), *twice(2, 7), *twice(7), *twice(3), *twice(3, 7), *twice(2),
+            *twice(4), *twice(2, 3), *twice(2, 7), *twice(7), *twice(3), *twice(3, 7), *twice(2),
         ],
         compiler_params=pltpu.CompilerParams(
             collective_id=0, has_side_effects=True, vmem_limit_bytes=56 * 2**20

time: 69 us -> 68.9 us (level)
  no operation moved by 1% of the time
where the time goes in v5:
time: 68.9 us; the launch traced here: 68.7 us
  Pallas kernels  68 us (99%)
    pallas_call x1, Pallas kernels, on_device(): pl.pallas_call(kernel, out_shape=shapes, in_specs=[pl.BlockSpec(memory_sp...  66.2 us
    pallas_call x1, Pallas kernels, on_device(): pl.pallas_call(hand_over, out_shape=shapes, in_specs=[pl.BlockSpec(memory...  1.85 us

profile of v5, /device:TPU:1, one launch (start us, length us, event | category | flops | bytes accessed | tf_op | source)
XLA Modules:
  0.0 68.7 jit_solution(15122602890181804850)
XLA Ops:
  0.6 66.2 %shard_map.67 = (bf16[160,1024]{1,0:T(8,128)(2,1)}, bf16[160,768]{1,0:T(8,128)(2,1)}, f32[32,768]{1,0:T(8,128)}) custom-call(bf16[160,1024]{1,0:T(8,128)(2,1)} %audio_hbm.1, bf16[160,768]{1,0:T(8,128)(2,1)} %text_hbm.1, s32[160]{0:T(256)} %labels_hbm.1, bf16[32,768]{1,0:T(8,128)(2,1)} %weight_hbm.1), custom_call_target="tpu_custom_call" | custom-call | tf_op jit(solution)/shard_map/pallas_call | solution.py:425
  66.8 1.9 %shard_map.68 = (bf16[160,1024]{1,0:T(8,128)(2,1)}, bf16[160,768]{1,0:T(8,128)(2,1)}, f32[32,768]{1,0:T(8,128)}) custom-call(bf16[160,1024]{1,0:T(8,128)(2,1)} %get-tuple-element.6.audio_in, bf16[160,768]{1,0:T(8,128)(2,1)} %get-tuple-element.7.text_in, f32[32,768]{1,0:T(8,128)} %get-tuple-element.8.grad_in), custom_call_target="tpu_custom_call" | custom-call | tf_op jit(solution)/shard_map/pallas_call | solution.py:476

commit v6 on v5

--- a/solution.py
+++ b/solution.py
@@ -12,7 +12,7 @@
 SHIFT = -4.0
 EPS = 1e-6
 ROWS, WIDE, COLS, HALF, MID = 160, 1024, 768, 80, 384
-AROUND = (1, 7, 2, 6, 3, 5, 4)
+AROUND = (4, 3, 5, 2, 6, 1, 7)
 
 
 def rows_by_columns(a, b):
@@ -331,13 +331,13 @@
     rs_send(2, 0)
     along_x()
     along_y(0)
+    along_y(1)
     along_y(2)
-    along_y(1)
     rs_send(1, 0)
 
     complete(0)
+    complete(1)
     complete(2)
-    complete(1)
 
     def final(to, k):
         return pltpu.make_async_remote_copy(

time: 68.9 us -> 68.9 us (level)
  no operation moved by 1% of the time
where the time goes in v6:
time: 68.9 us; the launch traced here: 68.7 us
  Pallas kernels  68.1 us (99%)
    pallas_call x1, Pallas kernels, on_device(): pl.pallas_call(kernel, out_shape=shapes, in_specs=[pl.BlockSpec(memory_sp...  66.2 us
    pallas_call x1, Pallas kernels, on_device(): pl.pallas_call(hand_over, out_shape=shapes, in_specs=[pl.BlockSpec(memory...  1.85 us

profile of v6, /device:TPU:1, one launch (start us, length us, event | category | flops | bytes accessed | tf_op | source)
XLA Modules:
  0.0 68.7 jit_solution(17752308928988436100)
XLA Ops:
  0.6 66.2 %shard_map.67 = (bf16[160,1024]{1,0:T(8,128)(2,1)}, bf16[160,768]{1,0:T(8,128)(2,1)}, f32[32,768]{1,0:T(8,128)}) custom-call(bf16[160,1024]{1,0:T(8,128)(2,1)} %audio_hbm.1, bf16[160,768]{1,0:T(8,128)(2,1)} %text_hbm.1, s32[160]{0:T(256)} %labels_hbm.1, bf16[32,768]{1,0:T(8,128)(2,1)} %weight_hbm.1), custom_call_target="tpu_custom_call" | custom-call | tf_op jit(solution)/shard_map/pallas_call | solution.py:425
  66.9 1.9 %shard_map.68 = (bf16[160,1024]{1,0:T(8,128)(2,1)}, bf16[160,768]{1,0:T(8,128)(2,1)}, f32[32,768]{1,0:T(8,128)}) custom-call(bf16[160,1024]{1,0:T(8,128)(2,1)} %get-tuple-element.6.audio_in, bf16[160,768]{1,0:T(8,128)(2,1)} %get-tuple-element.7.text_in, f32[32,768]{1,0:T(8,128)} %get-tuple-element.8.grad_in), custom_call_target="tpu_custom_call" | custom-call | tf_op jit(solution)/shard_map/pallas_call | solution.py:476
